TPU v7x, 512 devices: a whole 4x8x8 slice. The times are simulated.
512 devices in a mesh: dp: 8 (over z), table: 64 (over x, y, core).
Axes of the slice: x: 4, y: 8, z: 8, core: 2. Of those that a mesh axis runs over, the one named last changes fastest.
Arguments:
- lookups: int32 [524288, 13], P(('dp', 'table')), may hold values from 0 to 2047
- labels: int32 [524288], P(('dp', 'table')), may hold values 0 or 1
- replica: float32 [8, 1024, 128], P('dp'), may hold values from -6 to 6
- hot_state: float32 [8, 1024], P('dp'), may hold values from 0.001 to 0.1
- cold_table: float32 [32768, 128], P('table'), may hold values from -6 to 6
- cold_state: float32 [32768], P('table'), may hold values from 0.001 to 0.1
- w_hidden: bfloat16 [1664, 1024], replicated, may hold values from -0.15625 to 0.15625
- w_head: bfloat16 [1024], replicated, may hold values from -0.1875 to 0.1875
- requests: int32 [8, 64, 64, 16], P(None, 'table'), may hold values from 0 to 511, as said below
- tile_counts: int32 [64, 2], replicated, may hold values from 0 to 2, as said below
- demote_slots: int32 [64, 16], P('table'), may hold values from 0 to 1023, as said below
- demote_rows: int32 [64, 16], P('table'), may hold values from 0 to 511, as said below
- promote_slots: int32 [64, 16], replicated, may hold values from 0 to 1023, as said below
- promote_rows: int32 [64, 16], P('table'), may hold values from 0 to 511, as said below
Outputs:
- logits: float32 [524288], P(('dp', 'table'))
- replica_next: float32 [8, 1024, 128], P('dp')
- hot_state_next: float32 [8, 1024], P('dp')
- cold_next: float32 [32768, 128], P('table')
- cold_state_next: float32 [32768], P('table')
Inputs may be any that keep to these rules, and one draw needn't show every extreme that they name: requests[d, t, j, k] is a row local to table device t, never one of t's demote_rows. `tile_counts`: column 0 counts demoted tiles, column 1 promoted tiles; both columns reach 2 on some table device, and column 1 is column 0 reordered over table devices. `demote_slots`: entries i < 8 * tile_counts[t, 0] are live and distinct over all t; later entries are padding and unused. `demote_rows`: live entries as in demote_slots; distinct within a table device. `promote_slots`: entries i < 8 * tile_counts[t, 1] are live; the live promoted slots of all t are exactly the live demoted slots; later entries are padding. `promote_rows`: distinct within a table device and never one of its demote_rows.
All inputs are finite; a program needn't handle non-finite values. No bound on the sum of `labels` on one device may be relied on, other than what follows from the above.
Results may differ from a plain program's by a relative error of at most 0.003.
Values may be sent and summed in bfloat16 or wider, within the bound.
A program may use at most 64 MiB of HBM per device.

v0:
```python
import jax
import jax.numpy as jnp
from jax import lax
from jax.sharding import PartitionSpec as P

TILE = 8


learn_rate = 0.3


def adagrad(values, accum_state, row_grads):
    renewed = accum_state + jnp.mean(row_grads * row_grads, axis=-1)
    return (values - learn_rate * row_grads * lax.rsqrt(renewed)[..., None], renewed)


def dense_pass(embedded, labels, w_hidden, w_head):
    hidden = jnp.dot(embedded, w_hidden, preferred_element_type=jnp.float32)
    sigmoid_hidden = jax.nn.sigmoid(hidden)
    head_float = w_head.astype(jnp.float32)
    logits = jnp.sum(hidden * sigmoid_hidden * head_float, axis=1)
    residue = jax.nn.sigmoid(logits) - labels.astype(jnp.float32)
    silu_slope = sigmoid_hidden * (1.0 + hidden * (1.0 - sigmoid_hidden))
    hidden_grad = (residue[:, None] * head_float * silu_slope).astype(jnp.bfloat16)
    input_grad = lax.dot_general(
        hidden_grad, w_hidden, (((1,), (1,)), ((), ())), preferred_element_type=jnp.float32
    ).astype(jnp.bfloat16)
    return (logits, lax.optimization_barrier(input_grad))


def body(
    lookups,
    labels,
    replica,
    hot_state,
    cold_table,
    cold_state,
    w_hidden,
    w_head,
    requests,
    tile_counts,
    demote_slots,
    demote_rows,
    promote_slots,
    promote_rows,
):
    slot_count = replica.shape[1]
    row_width = replica.shape[2]
    own_rows = cold_table.shape[0]
    groups = lax.axis_size("dp")
    owners = lax.axis_size("table")
    owner_index = lax.axis_index("table")
    group_index = lax.axis_index("dp")
    capacity = requests.shape[3]
    padded_rows = demote_slots.shape[1]
    group_requests = lax.dynamic_index_in_dim(requests, group_index, 0, keepdims=False)[0]
    served = cold_table[group_requests].astype(jnp.bfloat16)
    fetched = lax.all_to_all(served, "table", split_axis=0, concat_axis=0, tiled=True)
    local_rows = jnp.concatenate(
        [replica[0].astype(jnp.bfloat16), fetched.reshape(-1, row_width)], axis=0
    )
    batch_rows, fields = lookups.shape
    flat_codes = lookups.reshape(-1)
    embedded = local_rows[flat_codes].reshape(batch_rows, fields * row_width)
    logits, input_grad = dense_pass(embedded, labels, w_hidden, w_head)
    slot_grads = jax.ops.segment_sum(
        input_grad.reshape(-1, row_width).astype(jnp.float32),
        flat_codes,
        num_segments=slot_count + owners * capacity,
    )
    hot_local = slot_grads[:slot_count]
    cold_local = slot_grads[slot_count:].reshape(owners, capacity, row_width)
    returned = lax.all_to_all(
        cold_local.astype(jnp.bfloat16), "table", split_axis=0, concat_axis=0, tiled=True
    ).astype(cold_local.dtype)
    hot_total = lax.psum(hot_local, "table")
    hot_rows, hot_accum = adagrad(replica[0], hot_state[0], hot_total)
    positions = jnp.arange(padded_rows, dtype=jnp.int32)
    own_counts = lax.dynamic_index_in_dim(tile_counts, owner_index, 0, keepdims=False)
    demote_live = positions < own_counts[0] * TILE
    demote_vals = hot_rows[demote_slots[0]]
    demote_accum = hot_accum[demote_slots[0]]
    dense_local = jax.ops.segment_sum(
        returned.reshape(-1, row_width), group_requests.reshape(-1), num_segments=own_rows
    )
    cold_grad, demote_total, accum_total = lax.psum((dense_local, demote_vals, demote_accum), "dp")
    cold_next, cold_state_next = adagrad(cold_table, cold_state, cold_grad)
    demote_index = jnp.where(demote_live, demote_rows[0], own_rows)
    cold_next = cold_next.at[demote_index].set(demote_total / groups, mode="drop")
    cold_state_next = cold_state_next.at[demote_index].set(accum_total / groups, mode="drop")
    send_rows = cold_next[promote_rows[0]]
    send_accum = cold_state_next[promote_rows[0]]
    every_rows, every_state = (
        lax.all_gather(send_rows, "table", axis=0, tiled=True),
        lax.all_gather(send_accum, "table", axis=0, tiled=True),
    )
    promote_live = (positions[None, :] < tile_counts[:, 1:2] * TILE).reshape(-1)
    slot_index = jnp.where(promote_live, promote_slots.reshape(-1), slot_count)
    replica_next = hot_rows.at[slot_index].set(every_rows, mode="drop")
    hot_state_next = hot_accum.at[slot_index].set(every_state, mode="drop")
    return (logits, replica_next[None], hot_state_next[None], cold_next, cold_state_next)


def solution(mesh):
    return jax.shard_map(
        body,
        mesh=mesh,
        in_specs=(
            P(("dp", "table"), None),
            P(("dp", "table")),
            P("dp", None, None),
            P("dp", None),
            P("table", None),
            P("table"),
            P(),
            P(),
            P(None, "table", None, None),
            P(),
            P("table", None),
            P("table", None),
            P(),
            P("table", None),
        ),
        out_specs=(
            P(("dp", "table")),
            P("dp", None, None),
            P("dp", None),
            P("table", None),
            P("table"),
        ),
        check_vma=False,
    )
```

profile of v0, /device:TPU:1, one launch (start us, length us, event | category | flops | bytes accessed | tf_op | source)
XLA Modules:
  0.0 673.7 jit_solution(16601498792197847210)
XLA Ops:
  8.1 0.9 compare_select_fusion.2
  8.9 0.1 copy.23
  9.0 0.1 reshape.239
  9.1 5.1 gather_fusion
  14.2 11.8 %all-to-all-start = ((bf16[64,16,128]{2,1,0:T(8,128)(2,1)}), bf16[64,16,128]{2,1,0:T(8,128)(2,1)}, u32[]{:S(2)}, u32[]{:S(2)}) async-start(bf16[64,16,128]{2,1,0:T(8,128)(2,1)} %bitcast.42), calls=%async_computation | async-start | bytes 524288 | tf_op jit(solution)/shard_map/all_to_all | solution.py:58
  26.0 1.9 copy.24
  27.9 1.4 reshape.230
  29.3 2.0 reshape.287
  31.3 1.8 bitcast_convert_fusion
  33.1 0.1 compare_select_fusion
  33.2 0.1 copy.26
  33.3 0.1 select_n.101
  33.4 0.1 constant_dynamic-slice_fusion
  33.5 0.5 slice.17
  34.7 3.2 all-to-all-done
  37.9 1.9 pad_maximum_fusion
  39.8 46.1 %gather_fusion.1 = bf16[13312,128]{1,0:T(8,128)(2,1)} fusion(bf16[2048,128]{1,0:T(8,128)(2,1)} %pad_maximum_fusion, s32[13312]{0:T(1024)S(1)} %broadcast_clamp_fusion), kind=kCustom, calls=%fused_computation.1 | custom fusion | bytes 6868992 | tf_op jit(solution)/shard_map/gather | solution.py:64
  85.8 7.5 %reshape.231 = bf16[1024,1664]{1,0:T(8,128)(2,1)} reshape(bf16[13312,128]{1,0:T(8,128)(2,1)} %gather_fusion.1) | data formatting | bytes 6815744 | tf_op jit(solution)/shard_map/reshape | solution.py:64
  93.3 6.9 %multiply_reduce_fusion = (f32[1024]{0:T(1024)S(1)}, f32[1024,1024]{0,1:T(8,128)S(1)}) fusion(f32[1024]{0:T(1024)S(1)} %convert_element_type.31, bf16[1024,1664]{1,0:T(8,128)(2,1)} %reshape.231, bf16[1664,1024]{1,0:T(8,128)(2,1)S(1)} %copy-done), kind=kOutput, calls=%fused_computation.13 | convolution fusion | flops 3495951360 | bytes 11018240 | tf_op jit(solution)/shard_map/dot_general | solution.py:18
  100.2 6.8 %convolution_convert_fusion = bf16[1024,1664]{1,0:T(8,128)(2,1)} fusion(bf16[1664,1024]{1,0:T(8,128)(2,1)S(1)} %copy-done, f32[1024,1024]{0,1:T(8,128)S(1)} %get-tuple-element.14, f32[1024]{0:T(1024)S(1)} %convert_subtract_fusion, f32[1024]{0:T(1024)S(1)} %convert_element_type.31), kind=kOutput, calls=%fused_computation.15 | convolution fusion | flops 3501850624 | bytes 11018240 | tf_op jit(solution)/shard_map/dot_general | solution.py:25
  107.0 7.8 %reshape.289 = f32[13312,128]{1,0:T(8,128)} reshape(bf16[1024,1664]{1,0:T(8,128)(2,1)} %convolution_convert_fusion) | data formatting | bytes 10223616 | tf_op jit(solution)/shard_map/convert_element_type | solution.py:67
  114.8 72.3 %scatter_custom_fusion = f32[2048,128]{1,0:T(8,128)} fusion(s32[13312]{0:T(1024)} %reshape.287, f32[13312,128]{1,0:T(8,128)} %reshape.289, f32[]{:T(128)} %constant.22.clone.1), kind=kCustom, calls=%fused_computation.26 | custom fusion | flops 1703936 | bytes 1049088 | tf_op jit(solution)/shard_map/scatter-add | solution.py:66
  187.1 1.9 slice.30
  189.1 1.8 slice.34
  190.8 7.3 %all-to-all-start.1 = ((bf16[64,16,128]{2,1,0:T(8,128)(2,1)}), bf16[64,16,128]{2,1,0:T(8,128)(2,1)}, u32[]{:S(2)}, u32[]{:S(2)}) async-start(bf16[64,16,128]{2,1,0:T(8,128)(2,1)} %bitcast.43), calls=%async_computation.1 | async-start | bytes 524288 | tf_op jit(solution)/shard_map/all_to_all | solution.py:73
  198.2 0.1 copy.27
  198.3 0.1 reshape.295
  198.4 1.3 dynamic-slice
  200.3 182.0 %all-reduce.5.cloned.1.call-done = f32[1024,128]{1,0:T(8,128)} async-done(((f32[1024,128]{1,0:T(8,128)}), f32[1024,128]{1,0:T(8,128)}) %all-reduce.5.cloned.1.call-update) | async-done | bytes 524304 | tf_op jit(solution)/shard_map/psum | solution.py:76
  382.4 1.2 multiply_reduce_fusion.1
  383.7 7.1 %scatter_custom_fusion.1 = f32[512,128]{1,0:T(8,128)} fusion(s32[1024]{0:T(1024)S(1)} %reshape.295, bf16[1024,128]{1,0:T(8,128)(2,1)} %bitcast.20, f32[]{:T(128)} %constant.22.clone.1), kind=kCustom, calls=%fused_computation.21 | custom fusion | flops 262144 | bytes 524292 | tf_op jit(solution)/shard_map/scatter-add | solution.py:83
  390.8 2.2 bitcast_subtract_fusion
  393.0 1.6 gather_fusion.2
  394.6 0.6 gather_fusion.4
  395.2 14.8 %all-reduce.1 = (f32[16,128]{1,0:T(8,128)S(1)}, f32[16]{0:T(128)S(1)}) all-reduce(f32[16,128]{1,0:T(8,128)S(1)} %gather_fusion.2, f32[16]{0:T(128)S(1)} %gather_fusion.4), channel_id=1, replica_groups=mesh['dp'=8,'table'=64] {'dp'}, use_global_device_ids=true, to_apply=%region_7.8 | all-reduce | flops 2064 | bytes 16512 | tf_op jit(solution)/shard_map/psum | solution.py:86
  410.1 53.9 %all-reduce.7.cloned.1.call-done = f32[512,128]{1,0:T(8,128)} async-done(((f32[512,128]{1,0:T(8,128)}), f32[512,128]{1,0:T(8,128)}) %all-reduce.7.cloned.1.call-update) | async-done | bytes 262160 | tf_op jit(solution)/shard_map/psum | solution.py:86
  463.9 1.1 multiply_reduce_fusion.2
  465.0 1.9 multiply_subtract_fusion
  466.9 2.2 scatter_custom_fusion.2
  469.2 1.5 gather_fusion.3
  470.7 60.3 %all-gather = f32[1024,128]{1,0:T(8,128)} all-gather(f32[16,128]{1,0:T(8,128)S(1)} %gather_fusion.3), channel_id=2, replica_groups=mesh['dp'=8,'table'=64] {'table'}, dimensions={0}, use_global_device_ids=true | all-gather | bytes 532480 | tf_op jit(solution)/shard_map/all_gather | solution.py:94
  531.0 0.6 scatter_fusion.1
  531.6 0.7 gather_fusion.5
  532.3 0.2 dynamic-update-slice
  532.5 123.6 %all-reduce = f32[1024]{0:T(1024)S(1)} all-reduce(f32[1024]{0:T(1024)S(1)} %dynamic-update-slice), channel_id=3, replica_groups=mesh['dp'=8,'table'=64] {'table'}, use_global_device_ids=true, to_apply=%add | all-reduce | flops 1024 | bytes 8192
  656.1 5.3 scatter_fusion
  661.4 4.3 scatter_fusion.2
  665.7 0.6 copy-done.1
  (46 shorter events, 0.3 us)
Async XLA Ops:
  8.0 85.3 %copy-start = (bf16[1664,1024]{1,0:T(8,128)(2,1)S(1)}, bf16[1664,1024]{1,0:T(8,128)(2,1)}, u32[]{:S(2)}) copy-start(bf16[1664,1024]{1,0:T(8,128)(2,1)} %param.20) | copy-start | bytes 10223620
  8.0 23.3 %copy-start.7 = (bf16[1024]{0:T(1024)(128)(2,1)S(1)}, bf16[1024]{0:T(1024)(128)(2,1)}, u32[]{:S(2)}) copy-start(bf16[1024]{0:T(1024)(128)(2,1)} %param.21) | copy-start | bytes 6148
  8.0 25.2 %copy-start.9 = (s32[64,2]{0,1:T(2,128)S(1)}, s32[64,2]{0,1:T(2,128)}, u32[]{:S(2)}) copy-start(s32[64,2]{0,1:T(2,128)} %param.23) | copy-start | bytes 1540
  8.0 25.2 %copy-start.3 = (s32[64,16]{0,1:T(8,128)S(1)}, s32[64,16]{0,1:T(8,128)}, u32[]{:S(2)}) copy-start(s32[64,16]{0,1:T(8,128)} %param.26) | copy-start | bytes 12292
  8.0 25.4 %copy-start.10 = (s32[1,16]{1,0:T(1,128)S(1)}, s32[1,16]{1,0:T(1,128)}, u32[]{:S(2)}) copy-start(s32[1,16]{1,0:T(1,128)} %param.24) | copy-start | bytes 196
  8.1 25.4 %copy-start.11 = (s32[1,16]{1,0:T(1,128)S(1)}, s32[1,16]{1,0:T(1,128)}, u32[]{:S(2)}) copy-start(s32[1,16]{1,0:T(1,128)} %param.27) | copy-start | bytes 196
  14.2 23.7 %all-to-all-start = ((bf16[64,16,128]{2,1,0:T(8,128)(2,1)}), bf16[64,16,128]{2,1,0:T(8,128)(2,1)}, u32[]{:S(2)}, u32[]{:S(2)}) async-start(bf16[64,16,128]{2,1,0:T(8,128)(2,1)} %bitcast.42), calls=%async_computation | async-start | bytes 524288 | tf_op jit(solution)/shard_map/all_to_all | solution.py:58
  26.0 356.4 %all-reduce.5.cloned.1.call-start = ((), (), s32[]{:S(2)}) async-start(), calls=%async_computation.2 | async-start | bytes 1048576 | tf_op jit(solution)/shard_map/psum | solution.py:76
  93.3 6.9 %copy-start.4 = (s32[1024]{0:T(1024)S(1)}, s32[1024]{0:T(1024)}, u32[]{:S(2)}) copy-start(s32[1024]{0:T(1024)} %param.15) | copy-start | bytes 12292
  100.2 6.8 %copy-start.5 = (f32[1024]{0:T(1024)}, f32[1024]{0:T(1024)S(1)}, u32[]{:S(2)}) copy-start(f32[1024]{0:T(1024)S(1)} %get-tuple-element.13) | copy-start | bytes 12292
  107.0 82.0 %copy-start.12 = (s32[1,16]{1,0:T(1,128)S(1)}, s32[1,16]{1,0:T(1,128)}, u32[]{:S(2)}) copy-start(s32[1,16]{1,0:T(1,128)} %param.25) | copy-start | bytes 196
  114.8 268.8 %copy-start.6 = (f32[1,1024]{1,0:T(1,128)S(1)}, f32[1,1024]{1,0:T(1,128)}, u32[]{:S(2)}) copy-start(f32[1,1024]{1,0:T(1,128)} %param.17) | copy-start | bytes 12292
  114.8 350.2 %copy-start.8 = (f32[512]{0:T(512)S(1)}, f32[512]{0:T(512)}, u32[]{:S(2)}) copy-start(f32[512]{0:T(512)} %param.19) | copy-start | bytes 6148
  190.8 192.8 %all-to-all-start.1 = ((bf16[64,16,128]{2,1,0:T(8,128)(2,1)}), bf16[64,16,128]{2,1,0:T(8,128)(2,1)}, u32[]{:S(2)}, u32[]{:S(2)}) async-start(bf16[64,16,128]{2,1,0:T(8,128)(2,1)} %bitcast.43), calls=%async_computation.1 | async-start | bytes 524288 | tf_op jit(solution)/shard_map/all_to_all | solution.py:73
  198.2 265.7 %all-reduce.7.cloned.1.call-start = ((), (), s32[]{:S(2)}) async-start(), calls=%async_computation.3 | async-start | bytes 524288 | tf_op jit(solution)/shard_map/psum | solution.py:86
  531.6 129.7 %copy-start.2 = (f32[512]{0:T(512)}, f32[512]{0:T(512)S(1)}, u32[]{:S(2)}) copy-start(f32[512]{0:T(512)S(1)} %scatter_fusion.1) | copy-start | bytes 6148
  665.7 0.6 copy-start.1
Sparse Core Ops, SparseCore 0:
  189.2 193.1 all-reduce.4
Sparse Core Ops, SparseCore 1:
  390.8 73.0 all-reduce.6
where the time goes:
time: 676 us; the launch traced here: 674 us
  waiting for transfers between devices  239 us (35%)
  blocking collectives  199 us (29%)
  local copies, waits for them, and re-layouts  93.2 us (14%)
  other arithmetic  92.7 us (14%)
  starting transfers between devices  19.2 us (3%)
  between operations  17.1 us (3%)
  matrix products  13.7 us (2%)
    psum x1, waiting for transfers between devices, body(): hot_total = lax.psum(hot_local, 'table')  182 us
    unnamed x1, blocking collectives  124 us
    scatter-add x1, other arithmetic, body(): jax.ops.segment_sum(input_grad.reshape(-1, row_width).astype(jnp.float32)...  72.3 us
    all_gather x1, blocking collectives, body(): lax.all_gather(send_rows, 'table', axis=0, tiled=True)  60.3 us
    psum x1, waiting for transfers between devices, body(): lax.psum((dense_local, demote_vals, demote_accum), 'dp')  53.9 us
    gather x1, local copies, waits for them, and re-layouts, body(): embedded = local_rows[flat_codes].reshape(batch_rows, fields * row_width)  46.1 us
    psum x1, blocking collectives, body(): lax.psum((dense_local, demote_vals, demote_accum), 'dp')  14.8 us
  transfers between devices with their start and end apart: 4, of which 3 were waited for; matrix products, arithmetic and copies ran while one was open for 3% of the time, Pallas kernels for 0%

commit v1 on v0

v1 whole, which is shorter than its diff:
```python
import functools

import jax
import jax.numpy as jnp
from jax import lax
from jax.experimental import pallas as pl
from jax.experimental.pallas import tpu as pltpu
from jax.sharding import PartitionSpec as P

MESH = pl.DeviceIdType.MESH
BF16 = jnp.bfloat16
F32 = jnp.float32
I32 = jnp.int32

TILE = 8
RATE = 0.3
LIMIT = 56 * 1024 * 1024


def vmem():
    return pl.BlockSpec(memory_space=pltpu.VMEM)


def smem():
    return pl.BlockSpec(memory_space=pltpu.SMEM)


def iota(shape, axis):
    return lax.broadcasted_iota(I32, shape, axis)


def ones_where(mask):
    return jnp.where(mask, 1.0, 0.0).astype(BF16)


def dot(a, b):
    return jnp.dot(a, b, preferred_element_type=F32)


def adagrad(values, accum_state, row_grads):
    renewed = accum_state + jnp.mean(row_grads * row_grads, axis=1, keepdims=True)
    return values - RATE * row_grads * lax.rsqrt(renewed), renewed


def column_of(scalars, rows, lanes, dtype):
    row = iota((rows, lanes), 0)
    out = jnp.zeros((rows, lanes), dtype)
    for i in range(rows):
        out = jnp.where(row == i, scalars(i), out)
    return out


def lanes_to_column(row):
    n = row.shape[1]
    return jnp.broadcast_to(row, (8, n)).T[:, :1]


def column_to_lanes(column):
    n = column.shape[0]
    return jnp.broadcast_to(column, (n, 128)).T[:1, :]


def wait_bytes(ref, sem):
    pltpu.make_async_copy(ref, ref, sem).wait()


def greet(axes):
    barrier = pltpu.get_barrier_semaphore()
    total = 0
    for axis in axes:
        n = lax.axis_size(axis)
        me = lax.axis_index(axis)

        def tell(o, carry, axis=axis, n=n, me=me):
            peer = lax.rem(me + o, n)
            pl.semaphore_signal(barrier, inc=1, device_id={axis: peer}, device_id_type=MESH)
            return carry

        lax.fori_loop(1, n, tell, 0)
        total += n - 1
    return barrier, total


def send_blocks(axis, src, dst, rows, per_peer, send_sem, recv_sem):
    n = lax.axis_size(axis)
    me = lax.axis_index(axis)

    def send(o, carry):
        peer = lax.rem(me + o, n)
        start = pl.multiple_of(peer * rows, rows) if per_peer else 0
        pltpu.make_async_remote_copy(
            src_ref=src.at[pl.ds(start, rows)],
            dst_ref=dst.at[pl.ds(pl.multiple_of(me * rows, rows), rows)],
            send_sem=send_sem,
            recv_sem=recv_sem,
            device_id={axis: peer},
            device_id_type=MESH,
        ).start()
        return carry

    lax.fori_loop(1, n, send, 0)


def own_block(axis, src, dst, rows, per_peer):
    me = lax.axis_index(axis)
    here = pl.ds(pl.multiple_of(me * rows, rows), rows)
    dst[here, :] = src[here, :] if per_peer else src[...]


def fetch_kernel(
    promote_rows, cold_state, requests, table, fetched, base, extra, onehot, served, base_own, extra_own, send_sem, recv_sem
):
    n = lax.axis_size("table")
    cap, width = requests.shape[2], table.shape[1]
    own = table.shape[0]
    pad = base_own.shape[0]
    barrier, greeted = greet(("table",))
    wanted = requests[lax.axis_index("dp"), 0]
    lane = iota((cap, own), 1)
    for j in range(n):
        onehot[j * cap : (j + 1) * cap, :] = ones_where(wanted[:, j : j + 1] == lane)
    served[...] = dot(onehot[...], table[...].astype(BF16)).astype(BF16)
    pl.semaphore_wait(barrier, greeted)
    send_blocks("table", served, fetched, cap, True, send_sem.at[0], recv_sem.at[0])
    for i in range(pad):
        base_own[i : i + 1, :] = table[pl.ds(promote_rows[0, i], 1), :]
    state = column_of(lambda i: cold_state[promote_rows[0, i]], pad, width, F32)
    high = state.astype(BF16)
    rest = state - high.astype(F32)
    mid = rest.astype(BF16)
    low = (rest - mid.astype(F32)).astype(BF16)
    place = iota((pad, width), 1)
    parts = jnp.where(place == 0, high.astype(F32), 0.0)
    parts = jnp.where(place == 1, mid.astype(F32), parts)
    parts = jnp.where(place == 2, low.astype(F32), parts)
    extra_own[...] = jnp.where(place == 3, 1.0, parts).astype(BF16)
    send_blocks("table", base_own, base, pad, False, send_sem.at[1], recv_sem.at[1])
    send_blocks("table", extra_own, extra, pad, False, send_sem.at[2], recv_sem.at[2])
    own_block("table", served, fetched, cap, True)
    own_block("table", base_own, base, pad, False)
    own_block("table", extra_own, extra, pad, False)
    got = pl.ds(0, (n - 1) * cap)
    for sem in (send_sem, recv_sem):
        wait_bytes(fetched.at[got], sem.at[0])
        wait_bytes(base.at[got], sem.at[1])
        wait_bytes(extra.at[got], sem.at[2])


def dense_kernel(
    lookups, labels, hot, fetched, w_hidden, w_head, logits, grads, codes, table, embedded, hots, masked, total, logit_column
):
    fields, batch = lookups.shape
    slots, width = hot.shape
    step = 256
    hidden_units = w_hidden.shape[1]
    blocks = slots // step
    for q in range(blocks):
        rows = pl.ds(q * step, step)
        table[:, q * width : (q + 1) * width] = hot[rows, :].astype(BF16)
        table[:, (blocks + q) * width : (blocks + q + 1) * width] = fetched[rows, :]
    padding = jnp.zeros((codes.shape[1] - fields - 1, batch), I32)
    codes[...] = jnp.concatenate([lookups[...], labels[...], padding], axis=0).T
    total[...] = jnp.zeros_like(total)
    span = masked.shape[1] // width
    group = total.shape[0]

    def tile(i, carry):
        rows = pl.ds(pl.multiple_of(i * step, step), step)
        lane = iota((step, step), 1)
        for f in range(fields):
            code = codes[rows, f : f + 1]
            found = dot(ones_where((code & (step - 1)) == lane), table[...])
            block = code // step
            entry = jnp.where(block == 0, found[:, :width], 0.0)
            for q in range(1, 2 * blocks):
                entry = jnp.where(block == q, found[:, q * width : (q + 1) * width], entry)
            embedded[:, f * width : (f + 1) * width] = entry.astype(BF16)
        hidden = dot(embedded[...], w_hidden[...])
        sig = jax.nn.sigmoid(hidden)
        head = w_head[...].astype(F32)
        logit = jnp.sum(hidden * sig * head, axis=1, keepdims=True)
        logit_column[rows, :] = logit
        residue = jax.nn.sigmoid(logit) - codes[rows, fields : fields + 1].astype(F32)
        slope = sig * (1.0 + hidden * (1.0 - sig))
        hidden_grad = (residue * head * slope).astype(BF16)
        input_grad = lax.dot_general(
            hidden_grad, w_hidden[...], (((1,), (1,)), ((), ())), preferred_element_type=F32
        )
        sub = iota((group, step), 0)
        for f in range(fields):
            grad = input_grad[:, f * width : (f + 1) * width].astype(BF16).astype(F32)
            block = codes[rows, f : f + 1] // group
            for q in range(span):
                masked[f * step : (f + 1) * step, q * width : (q + 1) * width] = jnp.where(
                    block == q, grad, 0.0
                ).astype(BF16)
            code = lookups[f : f + 1, rows] & (group - 1)
            hots[:, f * step : (f + 1) * step] = ones_where(code == sub)
        total[...] += dot(hots[...], masked[...])
        return carry

    lax.fori_loop(0, batch // step, tile, 0)
    logits[...] = column_to_lanes(logit_column[...])
    for q in range(span):
        grads[q * group : (q + 1) * group, :] = total[:, q * width : (q + 1) * width].astype(BF16)


def exchange_kernel(
    promote_rows,
    demote_slots,
    hot_state,
    requests,
    grads,
    replica,
    hot_grad,
    promo_grad,
    cold_grad,
    demoted,
    cold_back,
    hot_back,
    local,
    promo_own,
    demote_own,
    hot_own,
    cold_parts,
    promo_parts,
    cold_own,
    promo_sum,
    send_sem,
    recv_sem,
):
    n, groups = lax.axis_size("table"), lax.axis_size("dp")
    slots, width = replica.shape
    own = local.shape[0]
    cap = cold_back.shape[0] // n
    share = own // groups
    pad = promo_own.shape[0]
    barrier, greeted = greet(("table", "dp"))
    pl.semaphore_wait(barrier, greeted)
    hot_part, cold_part = grads.at[pl.ds(0, slots)], grads.at[pl.ds(slots, slots)]
    send_blocks("table", cold_part, cold_back, cap, True, send_sem.at[0], recv_sem.at[0])
    send_blocks("table", hot_part, hot_back, cap, True, send_sem.at[1], recv_sem.at[1])
    own_block("table", cold_part, cold_back, cap, True)
    own_block("table", hot_part, hot_back, cap, True)
    to_rows = ones_where(iota((own, n * cap), 0) == requests[...])
    demote_hot = ones_where(iota((pad, slots), 1) == column_of(lambda i: demote_slots[0, i], pad, slots, I32))
    for i in range(pad):
        demote_own[i : i + 1, :] = replica[pl.ds(demote_slots[0, i], 1), :]
    demote_state = column_of(lambda i: hot_state[0, demote_slots[0, i]], pad, width, F32)
    table_got = pl.ds(0, (n - 1) * cap)
    wait_bytes(cold_back.at[table_got], recv_sem.at[0])
    local[...] = dot(to_rows, cold_back[...])
    for i in range(pad):
        promo_own[i : i + 1, :] = local[pl.ds(promote_rows[0, i], 1), :]
    send_blocks("dp", promo_own, promo_parts, pad, False, send_sem.at[2], recv_sem.at[2])
    send_blocks("dp", local, cold_parts, share, True, send_sem.at[3], recv_sem.at[3])
    own_block("dp", promo_own, promo_parts, pad, False)
    me = lax.axis_index("dp")
    cold_parts[pl.ds(pl.multiple_of(me * share, share), share), :] = local[
        pl.ds(pl.multiple_of(me * share, share), share), :
    ]
    wait_bytes(hot_back.at[table_got], recv_sem.at[1])
    hot_sum = jnp.zeros((cap, width), F32)
    for j in range(n):
        hot_sum += hot_back[j * cap : (j + 1) * cap, :].astype(F32)
    hot_own[...] = hot_sum.astype(BF16)
    send_blocks("table", hot_own, hot_grad, cap, False, send_sem.at[4], recv_sem.at[4])
    own_block("table", hot_own, hot_grad, cap, False)
    wait_bytes(promo_parts.at[pl.ds(0, (groups - 1) * pad)], recv_sem.at[2])
    promo = promo_parts[0:pad, :]
    for g in range(1, groups):
        promo += promo_parts[g * pad : (g + 1) * pad, :]
    promo_sum[...] = promo.astype(BF16)
    send_blocks("table", promo_sum, promo_grad, pad, False, send_sem.at[5], recv_sem.at[5])
    own_block("table", promo_sum, promo_grad, pad, False)
    wait_bytes(cold_parts.at[pl.ds(0, (groups - 1) * share)], recv_sem.at[3])
    cold = cold_parts[0:share, :]
    for g in range(1, groups):
        cold += cold_parts[g * share : (g + 1) * share, :]
    cold_own[...] = cold.astype(BF16)
    send_blocks("dp", cold_own, cold_grad, share, False, send_sem.at[6], recv_sem.at[6])
    own_block("dp", cold_own, cold_grad, share, False)
    wait_bytes(hot_grad.at[table_got], recv_sem.at[4])
    demote_rows, demote_accum = adagrad(demote_own[0:pad, :], demote_state, dot(demote_hot, hot_grad[...]))
    demote_own[0:pad, :] = demote_rows
    demote_own[pad : 2 * pad, :] = demote_accum
    send_blocks("dp", demote_own, demoted, 2 * pad, False, send_sem.at[7], recv_sem.at[7])
    own_block("dp", demote_own, demoted, 2 * pad, False)
    dp_got = groups - 1
    wait_bytes(cold_grad.at[pl.ds(0, dp_got * share)], recv_sem.at[6])
    wait_bytes(promo_grad.at[table_got], recv_sem.at[5])
    wait_bytes(demoted.at[pl.ds(0, dp_got * 2 * pad)], recv_sem.at[7])
    wait_bytes(cold_back.at[table_got], send_sem.at[0])
    wait_bytes(hot_back.at[table_got], send_sem.at[1])
    wait_bytes(promo_parts.at[pl.ds(0, dp_got * pad)], send_sem.at[2])
    wait_bytes(cold_parts.at[pl.ds(0, dp_got * share)], send_sem.at[3])
    wait_bytes(hot_grad.at[table_got], send_sem.at[4])
    wait_bytes(promo_grad.at[table_got], send_sem.at[5])
    wait_bytes(cold_grad.at[pl.ds(0, dp_got * share)], send_sem.at[6])
    wait_bytes(demoted.at[pl.ds(0, dp_got * 2 * pad)], send_sem.at[7])


def update_kernel(
    tile_counts,
    demote_rows,
    promote_lanes,
    hot_grad,
    promo_grad,
    cold_grad,
    demoted,
    base,
    extra,
    replica,
    hot_state,
    table,
    cold_state,
    replica_next,
    hot_state_next,
    cold_next,
    cold_state_next,
    accum,
    *,
    groups,
):
    slots, width = replica.shape
    own = table.shape[0]
    pad = demoted.shape[0] // (2 * groups)
    values, renewed = adagrad(table[...], lanes_to_column(cold_state[...]), cold_grad[...].astype(F32))
    cold_next[...] = values
    accum[...] = jnp.broadcast_to(renewed, (own, width))
    mean = demoted[0 : 2 * pad, :]
    for g in range(1, groups):
        mean += demoted[2 * pad * g : 2 * pad * (g + 1), :]
    mean = mean / groups
    live = tile_counts[lax.axis_index("table"), 0] * TILE
    for i in range(pad):
        @pl.when(i < live)
        def _():
            cold_next[pl.ds(demote_rows[0, i], 1), :] = mean[i : i + 1, :]
            accum[pl.ds(demote_rows[0, i], 1), :] = mean[pad + i : pad + i + 1, :]

    cold_state_next[...] = accum[...].T[:1, :]
    pick = ones_where(iota((slots, promote_lanes.shape[1]), 0) == promote_lanes[...])
    value = base[...]
    high = value.astype(BF16)
    rest = value - high.astype(F32)
    mid = rest.astype(BF16)
    low = (rest - mid.astype(F32)).astype(BF16)
    chosen = dot(pick, jnp.concatenate([high, mid, low, extra[...], promo_grad[...]], axis=1))
    picked_value = (chosen[:, :width] + chosen[:, width : 2 * width]) + chosen[:, 2 * width : 3 * width]
    side = chosen[:, 3 * width : 4 * width]
    picked_state = (side[:, 0:1] + side[:, 1:2]) + side[:, 2:3]
    promoted = side[:, 3:4] > 0.0
    start = jnp.where(promoted, picked_value, replica[...])
    state = jnp.where(promoted, picked_state, lanes_to_column(hot_state[...]))
    grad = jnp.where(promoted, chosen[:, 4 * width :], hot_grad[...].astype(F32))
    values, renewed = adagrad(start, state, grad)
    replica_next[...] = values
    hot_state_next[...] = column_to_lanes(renewed)


def body(
    lookups,
    labels,
    replica,
    hot_state,
    cold_table,
    cold_state,
    w_hidden,
    w_head,
    requests,
    tile_counts,
    demote_slots,
    demote_rows,
    promote_slots,
    promote_rows,
):
    batch, fields = lookups.shape
    slots, width = replica.shape[1:]
    own = cold_table.shape[0]
    groups, n = lax.axis_size("dp"), lax.axis_size("table")
    cap = requests.shape[3]
    pad = demote_slots.shape[1]
    hidden_units = w_hidden.shape[1]
    dma = pltpu.SemaphoreType.DMA
    shape = jax.ShapeDtypeStruct

    fetched, base, extra = pl.pallas_call(
        fetch_kernel,
        out_shape=(
            shape((n * cap, width), BF16),
            shape((n * pad, width), F32),
            shape((n * pad, width), BF16),
        ),
        in_specs=[smem(), smem(), vmem(), vmem()],
        out_specs=(vmem(), vmem(), vmem()),
        scratch_shapes=[
            pltpu.VMEM((n * cap, own), BF16),
            pltpu.VMEM((n * cap, width), BF16),
            pltpu.VMEM((pad, width), F32),
            pltpu.VMEM((pad, width), BF16),
            dma((3,)),
            dma((3,)),
        ],
        compiler_params=pltpu.CompilerParams(collective_id=0, has_side_effects=True, vmem_limit_bytes=LIMIT),
        name="fetch",
    )(promote_rows, cold_state, requests.transpose(0, 1, 3, 2), cold_table)

    logits, grads = pl.pallas_call(
        dense_kernel,
        out_shape=(shape((1, batch), F32), shape((2 * slots, width), BF16)),
        in_specs=[vmem()] * 6,
        out_specs=(vmem(), vmem()),
        scratch_shapes=[
            pltpu.VMEM((batch, 16), I32),
            pltpu.VMEM((256, 8 * width), BF16),
            pltpu.VMEM((256, fields * width), BF16),
            pltpu.VMEM((512, fields * 256), BF16),
            pltpu.VMEM((fields * 256, 4 * width), BF16),
            pltpu.VMEM((512, 4 * width), F32),
            pltpu.VMEM((batch, 1), F32),
        ],
        compiler_params=pltpu.CompilerParams(vmem_limit_bytes=LIMIT),
        name="dense",
    )(
        lookups.T,
        labels.reshape(1, batch),
        replica[0],
        fetched,
        w_hidden,
        w_head.reshape(1, hidden_units),
    )

    wanted = lax.dynamic_index_in_dim(requests, lax.axis_index("dp"), 0, keepdims=False).reshape(1, n * cap)
    hot_grad, promo_grad, cold_grad, demoted = pl.pallas_call(
        exchange_kernel,
        out_shape=(
            shape((slots, width), BF16),
            shape((n * pad, width), BF16),
            shape((own, width), BF16),
            shape((groups * 2 * pad, width), F32),
        ),
        in_specs=[smem(), smem(), smem(), vmem(), vmem(), vmem()],
        out_specs=(vmem(), vmem(), vmem(), vmem()),
        scratch_shapes=[
            pltpu.VMEM((n * cap, width), BF16),
            pltpu.VMEM((slots, width), BF16),
            pltpu.VMEM((own, width), F32),
            pltpu.VMEM((pad, width), F32),
            pltpu.VMEM((2 * pad, width), F32),
            pltpu.VMEM((slots // n, width), BF16),
            pltpu.VMEM((own, width), F32),
            pltpu.VMEM((groups * pad, width), F32),
            pltpu.VMEM((own // groups, width), BF16),
            pltpu.VMEM((pad, width), BF16),
            dma((8,)),
            dma((8,)),
        ],
        compiler_params=pltpu.CompilerParams(collective_id=1, has_side_effects=True, vmem_limit_bytes=LIMIT),
        name="exchange",
    )(promote_rows, demote_slots, hot_state, wanted, grads, replica[0])

    positions = jnp.arange(pad, dtype=I32)
    live = positions[None, :] < tile_counts[:, 1:2] * TILE
    promote_lanes = jnp.where(live, promote_slots, -1).reshape(1, n * pad)
    replica_next, hot_state_next, cold_next, cold_state_next = pl.pallas_call(
        functools.partial(update_kernel, groups=groups),
        out_shape=(
            shape((slots, width), F32),
            shape((1, slots), F32),
            shape((own, width), F32),
            shape((1, own), F32),
        ),
        in_specs=[smem(), smem()] + [vmem()] * 11,
        out_specs=(vmem(), vmem(), vmem(), vmem()),
        scratch_shapes=[pltpu.VMEM((own, width), F32)],
        compiler_params=pltpu.CompilerParams(vmem_limit_bytes=LIMIT),
        name="update",
    )(
        tile_counts,
        demote_rows,
        promote_lanes,
        hot_grad,
        promo_grad,
        cold_grad,
        demoted,
        base,
        extra,
        replica[0],
        hot_state,
        cold_table,
        cold_state.reshape(1, own),
    )
    return (logits[0], replica_next[None], hot_state_next, cold_next, cold_state_next[0])


def solution(mesh):
    return jax.shard_map(
        body,
        mesh=mesh,
        in_specs=(
            P(("dp", "table"), None),
            P(("dp", "table")),
            P("dp", None, None),
            P("dp", None),
            P("table", None),
            P("table"),
            P(),
            P(),
            P(None, "table", None, None),
            P(),
            P("table", None),
            P("table", None),
            P(),
            P("table", None),
        ),
        out_specs=(
            P(("dp", "table")),
            P("dp", None, None),
            P("dp", None),
            P("table", None),
            P("table"),
        ),
        check_vma=False,
    )
```

time: 676 us -> 143 us (0.21)
  waiting for transfers between devices: 239 us -> 0 us
  blocking collectives: 199 us -> 0 us
  Pallas kernels: 0 us -> 136 us
  other arithmetic: 92.7 us -> 1.39 us
  local copies, waits for them, and re-layouts: 93.2 us -> 4.87 us
  starting transfers between devices: 19.2 us -> 0 us
  between operations: 17.1 us -> 0.66 us
  matrix products: 13.7 us -> 0 us
    psum x2 -> x0, waiting for transfers between devices: 236 us -> none  [the longest x1 182 us: body(): hot_total = lax.psum(hot_local, 'table')]
    pallas_call x0 -> x4, Pallas kernels: none -> 136 us  [the longest x1 45.4 us: body(): pl.pallas_call(exchange_kernel, out_shape=(shape((slots, width), BF16), s...]
    unnamed x1 -> x0, blocking collectives: 124 us -> none
    scatter-add x2 -> x0, other arithmetic: 79.4 us -> none  [the longest x1 72.3 us: body(): jax.ops.segment_sum(input_grad.reshape(-1, row_width).astype(jnp.float32)...]
    all_gather x1 -> x0, blocking collectives: 60.3 us -> none  [body(): lax.all_gather(send_rows, 'table', axis=0, tiled=True)]
    gather x6 -> x0, local copies, waits for them, and re-layouts: 55.6 us -> none  [the longest x1 46.1 us: body(): embedded = local_rows[flat_codes].reshape(batch_rows, fields * row_width)]
    all_to_all x2 -> x0, starting transfers between devices: 19.2 us -> none  [the longest x1 11.8 us: body(): lax.all_to_all(served, 'table', split_axis=0, concat_axis=0, tiled=True)]
    psum x1 -> x0, blocking collectives: 14.8 us -> none  [body(): lax.psum((dense_local, demote_vals, demote_accum), 'dp')]
  transfers between devices with their start and end apart: 4 -> 0, of which waited for: 3 -> 0; matrix products, arithmetic and copies ran while one was open for 3% -> 0% of each run, Pallas kernels for 0% -> 0%
where the time goes in v1:
time: 143 us
  Pallas kernels  136 us (95%)
  local copies, waits for them, and re-layouts  4.87 us (3%)
    pallas_call x1, Pallas kernels, body(): pl.pallas_call(exchange_kernel, out_shape=(shape((slots, width), BF16), s...  45.4 us
    pallas_call x1, Pallas kernels, body(): pl.pallas_call(dense_kernel, out_shape=(shape((1, batch), F32), shape((2...  43.7 us
    pallas_call x1, Pallas kernels, body(): pl.pallas_call(fetch_kernel, out_shape=(shape((n * cap, width), BF16), sh...  39.1 us
    pallas_call x1, Pallas kernels, body(): pl.pallas_call(functools.partial(update_kernel, groups=groups), out_shape...  7.43 us

profile of v1, /device:TPU:1, one launch (start us, length us, event | category | flops | bytes accessed | tf_op | source)
XLA Modules:
  0.0 142.6 jit_solution(17934620682721870698)
XLA Ops:
  0.6 0.7 multiply_bitcast_fusion
  1.3 1.3 reshape.27.w_head
  2.6 0.7 fusion
  3.3 0.7 constant_dynamic-slice_fusion
  4.0 0.1 copy.23
  4.1 0.7 reshape.29.requests
  4.8 0.1 copy.22
  4.8 0.7 reshape.28.promote_lanes
  5.5 1.4 copy.24.tile_counts
  6.9 39.1 %fetch.1 = (bf16[1024,128]{1,0:T(8,128)(2,1)}, f32[1024,128]{1,0:T(8,128)}, bf16[1024,128]{1,0:T(8,128)(2,1)}) custom-call(s32[1,16]{1,0:T(1,128)} %promote_rows.3, f32[512]{0:T(512)} %cold_state.1, s32[8,1,16,64]{3,2,1,0:T(8,128)} %bitcast.15, f32[512,128]{1,0:T(8,128)} %table.3), custom_call_target="tpu_custom_call" | custom-call | tf_op jit(solution)/shard_map/fetch/pallas_call | solution.py:388
  46.0 43.7 %dense.1 = (f32[1,1024]{1,0:T(1,128)}, bf16[2048,128]{1,0:T(8,128)(2,1)}) custom-call(s32[13,1024]{1,0:T(8,128)} %bitcast.16, s32[1,1024]{1,0:T(1,128)} %bitcast.18, f32[1024,128]{1,0:T(8,128)} %bitcast.12, bf16[1024,128]{1,0:T(8,128)(2,1)} %get-tuple-element.18.fetched, bf16[1664,1024]{1,0:T(8,128)(2,1)} %w_hidden.1, bf16[1,1024]{1,0:T(2,128)(2,1)} %reshape.27.w_head), custom_call_target="tpu_custom_call" | custom-call | tf_op jit(solution)/shard_map/dense/pallas_call | solution.py:409
  89.7 45.4 %exchange.1 = (bf16[1024,128]{1,0:T(8,128)(2,1)}, bf16[1024,128]{1,0:T(8,128)(2,1)}, bf16[512,128]{1,0:T(8,128)(2,1)}, f32[256,128]{1,0:T(8,128)}) custom-call(s32[1,16]{1,0:T(1,128)} %promote_rows.3, s32[1,16]{1,0:T(1,128)} %demote_slots.1, f32[1,1024]{1,0:T(1,128)} %hot_state.3, s32[1,1024]{1,0:T(1,128)} %reshape.29.requests, ...), custom_call_target="tpu_custom_call" | custom-call | tf_op jit(solution)/shard_map/exchange/pallas_call | solution.py:435
  135.1 7.4 %update.1 = (f32[1024,128]{1,0:T(8,128)}, f32[1,1024]{1,0:T(1,128)}, f32[512,128]{1,0:T(8,128)}, f32[1,512]{1,0:T(1,128)}) custom-call(s32[64,2]{1,0:T(8,128)} %copy.24.tile_counts, s32[1,16]{1,0:T(1,128)} %demote_rows.1, s32[1,1024]{1,0:T(1,128)} %reshape.28.promote_lanes, bf16[1024,128]{1,0:T(8,128)(2,1)} %get-tuple-element.21.hot_grad, ...), custom_call_target="tpu_custom_call" | custom-call | tf_op jit(solution)/shard_map/update/pallas_call | solution.py:466

commit v2 on v0

v2 whole, which is shorter than its diff:
```python
import functools

import jax
import jax.numpy as jnp
from jax import lax
from jax.experimental import pallas as pl
from jax.experimental.pallas import tpu as pltpu
from jax.sharding import PartitionSpec as P

MESH = pl.DeviceIdType.MESH
BF16 = jnp.bfloat16
F32 = jnp.float32
I32 = jnp.int32

TILE = 8
RATE = 0.3
LIMIT = 56 * 1024 * 1024


def vmem():
    return pl.BlockSpec(memory_space=pltpu.VMEM)


def smem():
    return pl.BlockSpec(memory_space=pltpu.SMEM)


def iota(shape, axis):
    return lax.broadcasted_iota(I32, shape, axis)


def one_hot(codes, shape, axis):
    index = iota(shape, axis).astype(jnp.int16)
    return jnp.where(codes.astype(jnp.int16) == index, jnp.ones(shape, BF16), jnp.zeros(shape, BF16))


def dot(a, b):
    return jnp.dot(a, b, preferred_element_type=F32)


def dot_lanes(a, b):
    return lax.dot_general(a, b, (((1,), (1,)), ((), ())), preferred_element_type=F32)


def split3(value):
    high = value.astype(BF16)
    rest = value - high.astype(F32)
    mid = rest.astype(BF16)
    return high, mid, (rest - mid.astype(F32)).astype(BF16)


def flat_lanes(array):
    n, k = array.shape
    per = 128 // k
    spread = jnp.concatenate([array] * per, axis=1)
    keep = iota((n, 128), 0) % per == iota((n, 128), 1) // k
    rows = jnp.sum(jnp.where(keep, spread, 0.0).reshape(n // per, per, 128), axis=1)
    return jnp.concatenate([rows[i : i + 1, :] for i in range(n // per)], axis=1)


def adagrad(values, accum_state, row_grads):
    renewed = accum_state + jnp.mean(row_grads * row_grads, axis=1, keepdims=True)
    return values - RATE * row_grads * lax.rsqrt(renewed), renewed


def column_of(scalars, rows, lanes, dtype):
    row = iota((rows, lanes), 0)
    out = jnp.zeros((rows, lanes), dtype)
    for i in range(rows):
        out = jnp.where(row == i, scalars(i), out)
    return out


def lanes_to_column(row):
    n = row.shape[1]
    return jnp.broadcast_to(row, (8, n)).T[:, :1]


def column_to_lanes(column):
    n = column.shape[0]
    return jnp.broadcast_to(column, (n, 128)).T[:1, :]


def wait_bytes(ref, sem):
    pltpu.make_async_copy(ref, ref, sem).wait()


def greet(axes):
    barrier = pltpu.get_barrier_semaphore()
    total = 0
    for axis in axes:
        n = lax.axis_size(axis)
        me = lax.axis_index(axis)

        def tell(o, carry, axis=axis, n=n, me=me):
            peer = lax.rem(me + o, n)
            pl.semaphore_signal(barrier, inc=1, device_id={axis: peer}, device_id_type=MESH)
            return carry

        lax.fori_loop(1, n, tell, 0)
        total += n - 1
    return barrier, total


def send_blocks(axis, src, dst, rows, per_peer, send_sem, recv_sem):
    n = lax.axis_size(axis)
    me = lax.axis_index(axis)

    def send(o, carry):
        peer = lax.rem(me + o, n)
        start = pl.multiple_of(peer * rows, rows) if per_peer else 0
        pltpu.make_async_remote_copy(
            src_ref=src.at[pl.ds(start, rows)],
            dst_ref=dst.at[pl.ds(pl.multiple_of(me * rows, rows), rows)],
            send_sem=send_sem,
            recv_sem=recv_sem,
            device_id={axis: peer},
            device_id_type=MESH,
        ).start()
        return carry

    lax.fori_loop(1, n, send, 0)


def own_block(axis, src, dst, rows, per_peer):
    me = lax.axis_index(axis)
    here = pl.ds(pl.multiple_of(me * rows, rows), rows)
    dst[here, :] = src[here, :] if per_peer else src[...]


def step_kernel(
    promote_rows,
    demote_rows,
    demote_slots,
    cold_state_scalars,
    hot_state_scalars,
    lookups,
    labels,
    replica,
    hot_state,
    cold_table,
    cold_state,
    w_hbm,
    w_head,
    requests,
    tile_counts,
    promote_slots,
    logits,
    replica_next,
    hot_state_next,
    cold_next,
    cold_state_next,
    w_hidden,
    w_flipped,
    wanted_rows,
    served,
    fetched,
    base_own,
    base,
    state_own,
    states,
    table,
    rows,
    cold_send,
    hot_send,
    cold_back,
    hot_back,
    local,
    promo_own,
    demote_own,
    hot_own,
    cold_parts,
    promo_parts,
    cold_own,
    promo_sum,
    hot_grad,
    promo_grad,
    cold_grad,
    demoted,
    pick,
    start,
    w_sem,
    send_sem,
    recv_sem,
):
    n, groups = lax.axis_size("table"), lax.axis_size("dp")
    me, group = lax.axis_index("table"), lax.axis_index("dp")
    fields, batch = lookups.shape
    slots, width = replica.shape
    own = cold_table.shape[0]
    cap, pad = requests.shape[2], demote_slots.shape[1]
    share = own // groups
    half = table.shape[1]
    blocks = slots // half
    table_got = pl.ds(0, (n - 1) * cap)
    dp_got = groups - 1

    load = pltpu.make_async_copy(w_hbm, w_hidden, w_sem)
    load.start()
    barrier, greeted = greet(("table", "dp"))

    wanted = requests[group, 0]
    for j in range(n):
        wanted_rows[j * cap : (j + 1) * cap, :] = one_hot(wanted[:, j : j + 1], (cap, own), 1)
    served[...] = dot(wanted_rows[...], cold_table[...].astype(BF16)).astype(BF16)
    pl.semaphore_wait(barrier, greeted)
    send_blocks("table", served, fetched, cap, True, send_sem.at[0], recv_sem.at[0])
    own_block("table", served, fetched, cap, True)

    for q in range(blocks):
        table[q * width : (q + 1) * width, :] = replica[q * half : (q + 1) * half, :].T.astype(BF16)
    for f in range(fields):
        code = lookups[f : f + 1, :]
        found = dot(table[...], one_hot(code & (half - 1), (half, batch), 0))
        block = code >> (half.bit_length() - 1)
        entry = jnp.where(block == 0, found[:width, :], 0.0)
        for q in range(1, blocks):
            entry = jnp.where(block == q, found[q * width : (q + 1) * width, :], entry)
        rows[f * width : (f + 1) * width, :] = entry.astype(BF16)
    load.wait()
    for f in range(fields):
        part = slice(f * width, (f + 1) * width)
        w_flipped[:, part] = w_hidden[part, :].T
    head = jnp.broadcast_to(w_head[...].astype(F32), (width, w_head.shape[1])).T
    for i in range(pad):
        base_own[i : i + 1, :] = cold_table[pl.ds(promote_rows[0, i], 1), :]
    place = iota((8, width), 1)
    state = jnp.zeros((8, width), F32)
    for i in range(pad):
        state = jnp.where(place == i, cold_state_scalars[promote_rows[0, i]], state)
    state_own[...] = state

    wait_bytes(fetched.at[table_got], recv_sem.at[0])
    send_blocks("table", base_own, base, pad, False, send_sem.at[1], recv_sem.at[1])
    send_blocks("table", state_own, states, 8, False, send_sem.at[2], recv_sem.at[2])
    own_block("table", base_own, base, pad, False)
    own_block("table", state_own, states, 8, False)
    for q in range(blocks):
        table[q * width : (q + 1) * width, :] = fetched[q * half : (q + 1) * half, :].astype(F32).T.astype(BF16)
    for f in range(fields):
        code = lookups[f : f + 1, :]
        found = dot(table[...], one_hot(code & (half - 1), (half, batch), 0))
        block = code >> (half.bit_length() - 1)
        entry = rows[f * width : (f + 1) * width, :].astype(F32)
        for q in range(blocks):
            entry = jnp.where(block == blocks + q, found[q * width : (q + 1) * width, :], entry)
        rows[f * width : (f + 1) * width, :] = entry.astype(BF16)

    hidden = dot(w_flipped[...], rows[...])
    sig = jax.nn.sigmoid(hidden)
    heads = jnp.concatenate([head] * (batch // width), axis=1)
    logit = jnp.sum(hidden * sig * heads, axis=0, keepdims=True)
    logits[...] = logit
    residue = jax.nn.sigmoid(logit) - labels[...].astype(F32)
    slope = sig * (1.0 + hidden * (1.0 - sig))
    hidden_grad = (residue * heads * slope).astype(BF16)
    rows[...] = dot(w_hidden[...], hidden_grad).astype(BF16)

    def summed(first, out):
        total = jnp.zeros((half, blocks * width), F32)
        for f in range(fields):
            code = lookups[f : f + 1, :]
            block = code >> (half.bit_length() - 1)
            grad = rows[f * width : (f + 1) * width, :].astype(F32)
            masked = jnp.concatenate(
                [jnp.where(block == first + q, grad, 0.0).astype(BF16) for q in range(blocks)], axis=0
            )
            total += dot_lanes(one_hot(code & (half - 1), (half, batch), 0), masked)
        for q in range(blocks):
            out[q * half : (q + 1) * half, :] = total[:, q * width : (q + 1) * width].astype(BF16)

    summed(blocks, cold_send)
    send_blocks("table", cold_send, cold_back, cap, True, send_sem.at[3], recv_sem.at[3])
    own_block("table", cold_send, cold_back, cap, True)
    summed(0, hot_send)
    send_blocks("table", hot_send, hot_back, cap, True, send_sem.at[4], recv_sem.at[4])
    own_block("table", hot_send, hot_back, cap, True)

    to_rows = one_hot(flat_lanes(wanted.astype(F32).T).astype(I32), (own, n * cap), 0)
    demote_hot = one_hot(column_of(lambda i: demote_slots[0, i], pad, slots, I32), (pad, slots), 1)
    for i in range(pad):
        demote_own[i : i + 1, :] = replica[pl.ds(demote_slots[0, i], 1), :]
    demote_state = column_of(lambda i: hot_state_scalars[0, demote_slots[0, i]], pad, width, F32)
    counts = tile_counts[...]
    live = iota((pad, n), 0) < counts[1:2, :] * TILE
    targets = flat_lanes(jnp.where(live, promote_slots[...], slots).astype(F32).T).astype(I32)
    pick[...] = one_hot(targets, (slots, n * pad), 0)
    wait_bytes(base.at[table_got], recv_sem.at[1])
    wait_bytes(states.at[pl.ds(0, (n - 1) * 8)], recv_sem.at[2])
    chosen = dot(pick[...], jnp.concatenate(split3(base[...]), axis=1))
    picked = (chosen[:, :width] + chosen[:, width : 2 * width]) + chosen[:, 2 * width :]
    state_lanes = flat_lanes(states[...].reshape(n, 8, width)[:, 0, :pad])
    pieces = [piece.astype(F32) for piece in split3(state_lanes)]
    side_rows = jnp.concatenate(pieces + [jnp.ones_like(state_lanes)] + [jnp.zeros_like(state_lanes)] * 4, axis=0)
    side = dot_lanes(pick[...], side_rows.astype(BF16))
    promoted = side[:, 3:4] > 0.0
    start[...] = jnp.where(promoted, picked, replica[...])
    start_state = jnp.where(promoted, (side[:, 0:1] + side[:, 1:2]) + side[:, 2:3], lanes_to_column(hot_state[...]))
    cold_column = lanes_to_column(cold_state[...])

    wait_bytes(cold_back.at[table_got], recv_sem.at[3])
    local[...] = dot(to_rows, cold_back[...])
    for i in range(pad):
        promo_own[i : i + 1, :] = local[pl.ds(promote_rows[0, i], 1), :]
    send_blocks("dp", promo_own, promo_parts, pad, False, send_sem.at[5], recv_sem.at[5])
    send_blocks("dp", local, cold_parts, share, True, send_sem.at[6], recv_sem.at[6])
    own_block("dp", promo_own, promo_parts, pad, False)
    own_block("dp", local, cold_parts, share, True)
    wait_bytes(hot_back.at[table_got], recv_sem.at[4])
    hot_own[...] = jnp.sum(hot_back[...].astype(F32).reshape(n, cap, width), axis=0).astype(BF16)
    send_blocks("table", hot_own, hot_grad, cap, False, send_sem.at[7], recv_sem.at[7])
    own_block("table", hot_own, hot_grad, cap, False)
    wait_bytes(promo_parts.at[pl.ds(0, dp_got * pad)], recv_sem.at[5])
    promo_sum[...] = jnp.sum(promo_parts[...].reshape(groups, pad, width), axis=0).astype(BF16)
    send_blocks("table", promo_sum, promo_grad, pad, False, send_sem.at[8], recv_sem.at[8])
    own_block("table", promo_sum, promo_grad, pad, False)
    wait_bytes(cold_parts.at[pl.ds(0, dp_got * share)], recv_sem.at[6])
    cold_own[...] = jnp.sum(cold_parts[...].reshape(groups, share, width), axis=0).astype(BF16)
    send_blocks("dp", cold_own, cold_grad, share, False, send_sem.at[9], recv_sem.at[9])
    own_block("dp", cold_own, cold_grad, share, False)
    wait_bytes(hot_grad.at[table_got], recv_sem.at[7])
    values, renewed = adagrad(demote_own[0:pad, :], demote_state, dot(demote_hot, hot_grad[...]))
    demote_own[0:pad, :] = values
    demote_own[pad : 2 * pad, :] = renewed
    send_blocks("dp", demote_own, demoted, 2 * pad, False, send_sem.at[10], recv_sem.at[10])
    own_block("dp", demote_own, demoted, 2 * pad, False)
    wait_bytes(cold_grad.at[pl.ds(0, dp_got * share)], recv_sem.at[9])
    values, renewed = adagrad(cold_table[...], cold_column, cold_grad[...].astype(F32))
    wait_bytes(promo_grad.at[table_got], recv_sem.at[8])
    grad = jnp.where(promoted, dot(pick[...], promo_grad[...]), hot_grad[...].astype(F32))
    hot_values, hot_renewed = adagrad(start[...], start_state, grad)
    replica_next[...] = hot_values
    hot_state_next[...] = column_to_lanes(hot_renewed)
    wait_bytes(demoted.at[pl.ds(0, dp_got * 2 * pad)], recv_sem.at[10])
    mean = jnp.sum(demoted[...].reshape(groups, 2 * pad, width), axis=0) / groups
    renewed = jnp.broadcast_to(renewed, (own, width))
    count = jnp.sum(jnp.where(iota((1, n), 1) == me, counts[0:1, :], 0), axis=1, keepdims=True) * TILE
    row = iota((own, width), 0)
    for i in range(pad):
        here = (row == demote_rows[0, i]) & (i < count)
        values = jnp.where(here, mean[i : i + 1, :], values)
        renewed = jnp.where(here, mean[pad + i : pad + i + 1, :], renewed)
    cold_next[...] = values
    cold_state_next[...] = renewed.T[:1, :]

    wait_bytes(fetched.at[table_got], send_sem.at[0])
    wait_bytes(base.at[table_got], send_sem.at[1])
    wait_bytes(states.at[pl.ds(0, (n - 1) * 8)], send_sem.at[2])
    wait_bytes(cold_back.at[table_got], send_sem.at[3])
    wait_bytes(hot_back.at[table_got], send_sem.at[4])
    wait_bytes(promo_parts.at[pl.ds(0, dp_got * pad)], send_sem.at[5])
    wait_bytes(cold_parts.at[pl.ds(0, dp_got * share)], send_sem.at[6])
    wait_bytes(hot_grad.at[table_got], send_sem.at[7])
    wait_bytes(promo_grad.at[table_got], send_sem.at[8])
    wait_bytes(cold_grad.at[pl.ds(0, dp_got * share)], send_sem.at[9])
    wait_bytes(demoted.at[pl.ds(0, dp_got * 2 * pad)], send_sem.at[10])


def body(
    lookups,
    labels,
    replica,
    hot_state,
    cold_table,
    cold_state,
    w_hidden,
    w_head,
    requests,
    tile_counts,
    demote_slots,
    demote_rows,
    promote_slots,
    promote_rows,
):
    batch, fields = lookups.shape
    slots, width = replica.shape[1:]
    own = cold_table.shape[0]
    groups, n = lax.axis_size("dp"), lax.axis_size("table")
    cap = requests.shape[3]
    pad = demote_slots.shape[1]
    inputs, units = w_hidden.shape
    dma = pltpu.SemaphoreType.DMA
    shape = jax.ShapeDtypeStruct
    logits, replica_next, hot_state_next, cold_next, cold_state_next = pl.pallas_call(
        step_kernel,
        out_shape=(
            shape((1, batch), F32),
            shape((slots, width), F32),
            shape((1, slots), F32),
            shape((own, width), F32),
            shape((1, own), F32),
        ),
        in_specs=[smem()] * 5 + [vmem()] * 6 + [pl.BlockSpec(memory_space=pl.ANY)] + [vmem()] * 4,
        out_specs=(vmem(),) * 5,
        scratch_shapes=[
            pltpu.VMEM((inputs, units), BF16),
            pltpu.VMEM((units, inputs), BF16),
            pltpu.VMEM((n * cap, own), BF16),
            pltpu.VMEM((n * cap, width), BF16),
            pltpu.VMEM((n * cap, width), BF16),
            pltpu.VMEM((pad, width), F32),
            pltpu.VMEM((n * pad, width), F32),
            pltpu.VMEM((8, width), F32),
            pltpu.VMEM((n * 8, width), F32),
            pltpu.VMEM((2 * width, 512), BF16),
            pltpu.VMEM((inputs, batch), BF16),
            pltpu.VMEM((n * cap, width), BF16),
            pltpu.VMEM((slots, width), BF16),
            pltpu.VMEM((n * cap, width), BF16),
            pltpu.VMEM((slots, width), BF16),
            pltpu.VMEM((own, width), F32),
            pltpu.VMEM((pad, width), F32),
            pltpu.VMEM((2 * pad, width), F32),
            pltpu.VMEM((slots // n, width), BF16),
            pltpu.VMEM((own, width), F32),
            pltpu.VMEM((groups * pad, width), F32),
            pltpu.VMEM((own // groups, width), BF16),
            pltpu.VMEM((pad, width), BF16),
            pltpu.VMEM((slots, width), BF16),
            pltpu.VMEM((n * pad, width), BF16),
            pltpu.VMEM((own, width), BF16),
            pltpu.VMEM((groups * 2 * pad, width), F32),
            pltpu.VMEM((slots, n * pad), BF16),
            pltpu.VMEM((slots, width), F32),
            dma,
            dma((11,)),
            dma((11,)),
        ],
        compiler_params=pltpu.CompilerParams(collective_id=0, has_side_effects=True, vmem_limit_bytes=LIMIT),
        name="step",
    )(
        promote_rows,
        demote_rows,
        demote_slots,
        cold_state,
        hot_state,
        lookups.T,
        labels.reshape(1, batch),
        replica[0],
        hot_state,
        cold_table,
        cold_state.reshape(1, own),
        w_hidden,
        w_head.reshape(1, units),
        requests.transpose(0, 1, 3, 2),
        tile_counts.T,
        promote_slots.T,
    )
    return (logits[0], replica_next[None], hot_state_next, cold_next, cold_state_next[0])


def solution(mesh):
    return jax.shard_map(
        body,
        mesh=mesh,
        in_specs=(
            P(("dp", "table"), None),
            P(("dp", "table")),
            P("dp", None, None),
            P("dp", None),
            P("table", None),
            P("table"),
            P(),
            P(),
            P(None, "table", None, None),
            P(),
            P("table", None),
            P("table", None),
            P(),
            P("table", None),
        ),
        out_specs=(
            P(("dp", "table")),
            P("dp", None, None),
            P("dp", None),
            P("table", None),
            P("table"),
        ),
        check_vma=False,
    )
```

time: 676 us -> 93.4 us (0.14)
  waiting for transfers between devices: 239 us -> 0 us
  blocking collectives: 199 us -> 0 us
  other arithmetic: 92.7 us -> 0 us
  local copies, waits for them, and re-layouts: 93.2 us -> 8.59 us
  Pallas kernels: 0 us -> 83.8 us
  starting transfers between devices: 19.2 us -> 0 us
  between operations: 17.1 us -> 0.64 us
  matrix products: 13.7 us -> 0 us
    psum x2 -> x0, waiting for transfers between devices: 236 us -> none  [the longest x1 182 us: body(): hot_total = lax.psum(hot_local, 'table')]
    unnamed x1 -> x0, blocking collectives: 124 us -> none
    pallas_call x0 -> x1, Pallas kernels: none -> 83.8 us  [body(): pl.pallas_call(step_kernel, out_shape=(shape((1, batch), F32), shape((slo...]
    scatter-add x2 -> x0, other arithmetic: 79.4 us -> none  [the longest x1 72.3 us: body(): jax.ops.segment_sum(input_grad.reshape(-1, row_width).astype(jnp.float32)...]
    all_gather x1 -> x0, blocking collectives: 60.3 us -> none  [body(): lax.all_gather(send_rows, 'table', axis=0, tiled=True)]
    gather x6 -> x0, local copies, waits for them, and re-layouts: 55.6 us -> none  [the longest x1 46.1 us: body(): embedded = local_rows[flat_codes].reshape(batch_rows, fields * row_width)]
    all_to_all x2 -> x0, starting transfers between devices: 19.2 us -> none  [the longest x1 11.8 us: body(): lax.all_to_all(served, 'table', split_axis=0, concat_axis=0, tiled=True)]
    psum x1 -> x0, blocking collectives: 14.8 us -> none  [body(): lax.psum((dense_local, demote_vals, demote_accum), 'dp')]
  transfers between devices with their start and end apart: 4 -> 0, of which waited for: 3 -> 0; matrix products, arithmetic and copies ran while one was open for 3% -> 0% of each run, Pallas kernels for 0% -> 0%
where the time goes in v2:
time: 93.4 us; the launch traced here: 93 us
  Pallas kernels  83.8 us (90%)
  local copies, waits for them, and re-layouts  8.59 us (9%)
    pallas_call x1, Pallas kernels, body(): pl.pallas_call(step_kernel, out_shape=(shape((1, batch), F32), shape((slo...  83.8 us
    unnamed x5, local copies, waits for them, and re-layouts  7.31 us

profile of v2, /device:TPU:1, one launch (start us, length us, event | category | flops | bytes accessed | tf_op | source)
XLA Modules:
  0.0 93.0 jit_solution(8879989289951817194)
XLA Ops:
  0.6 1.3 %reshape.21.w_head = bf16[1,1024]{1,0:T(2,128)(2,1)} reshape(bf16[1024]{0:T(1024)(128)(2,1)} %param.21) | data formatting | bytes 4096 | tf_op jit(solution)/shard_map/reshape | solution.py:444
  1.9 83.8 %step.1 = (f32[1,1024]{1,0:T(1,128)}, f32[1024,128]{1,0:T(8,128)}, f32[1,1024]{1,0:T(1,128)}, f32[512,128]{1,0:T(8,128)}, f32[1,512]{1,0:T(1,128)}) custom-call(s32[1,16]{1,0:T(1,128)} %promote_rows.1, s32[1,16]{1,0:T(1,128)} %demote_rows.1, s32[1,16]{1,0:T(1,128)} %demote_slots.1, f32[512]{0:T(512)} %cold_state_scalars.1, f32[1,1024]{1,0:T(1,128)} %hot_state.1, ...), custom_call_target="tpu_custom_call" | custom-call | tf_op jit(solution)/shard_map/step/pallas_call | solution.py:384
  85.7 1.3 %copy.24 = f32[1024]{0:T(1024)} copy(f32[1024]{0:T(1024)} %bitcast.17) | data formatting | bytes 8192
  87.0 1.9 %copy.25 = f32[1,1024,128]{2,1,0:T(8,128)} copy(f32[1,1024,128]{2,1,0:T(8,128)} %bitcast.11) | data formatting | bytes 1048576
  88.9 1.3 %copy.26 = f32[1,1024]{1,0:T(1,128)} copy(f32[1,1024]{1,0:T(1,128)} %get-tuple-element.22) | data formatting | bytes 8192
  90.1 1.7 %copy.27 = f32[512,128]{1,0:T(8,128)} copy(f32[512,128]{1,0:T(8,128)} %get-tuple-element.23) | data formatting | bytes 524288
  91.8 1.2 %copy.28 = f32[512]{0:T(512)} copy(f32[512]{0:T(512)} %bitcast.18) | data formatting | bytes 4096

commit v3 on v2

--- a/solution.py
+++ b/solution.py
@@ -126,6 +126,90 @@
     me = lax.axis_index(axis)
     here = pl.ds(pl.multiple_of(me * rows, rows), rows)
     dst[here, :] = src[here, :] if per_peer else src[...]
+
+
+Y = 8
+
+
+def remote(src, dst, sems, peer):
+    pltpu.make_async_remote_copy(
+        src_ref=src, dst_ref=dst, send_sem=sems[0], recv_sem=sems[1], device_id={"table": peer}, device_id_type=MESH
+    ).start()
+
+
+def block_of(index, chips):
+    return lax.rem(index, 2) * chips + index // 2
+
+
+def some_rows(first, count, rows):
+    return pl.ds(pl.multiple_of(first * rows, rows), count * rows)
+
+
+def scatter_by_core(src, dst, rows, sems):
+    n = lax.axis_size("table")
+    me = lax.axis_index("table")
+    here = some_rows(block_of(me, n // 2), 1, rows)
+
+    def send(o, carry):
+        peer = lax.rem(me + o, n)
+        remote(src.at[some_rows(block_of(peer, n // 2), 1, rows)], dst.at[here], sems, peer)
+        return carry
+
+    lax.fori_loop(1, n, send, 0)
+    dst[here, :] = src[here, :]
+
+
+def gather_same_core(src, dst, rows, sems):
+    n = lax.axis_size("table")
+    me = lax.axis_index("table")
+    chips = n // 2
+    core, chip = lax.rem(me, 2), me // 2
+    here = some_rows(block_of(me, chips), 1, rows)
+
+    def send(o, carry):
+        remote(src, dst.at[here], sems, lax.rem(chip + o, chips) * 2 + core)
+        return carry
+
+    lax.fori_loop(1, chips, send, 0)
+    dst[here, :] = src[...]
+
+
+def gather_other_core(dst, rows, sems):
+    chips = lax.axis_size("table") // 2
+    me = lax.axis_index("table")
+    core = lax.rem(me, 2)
+    half = some_rows(core * chips, chips, rows)
+    remote(dst.at[half], dst.at[half], sems, me + 1 - 2 * core)
+
+
+def gather_along_y(src, dst, rows, sems):
+    n = lax.axis_size("table")
+    me = lax.axis_index("table")
+    core, chip = lax.rem(me, 2), me // 2
+    here = some_rows(block_of(me, n // 2), 1, rows)
+    for o in range(1, Y):
+        peer = (chip // Y * Y + lax.rem(lax.rem(chip, Y) + o, Y)) * 2 + core
+        remote(src, dst.at[here], sems, peer)
+    dst[here, :] = src[...]
+
+
+def gather_along_x(dst, rows, sems):
+    n = lax.axis_size("table")
+    me = lax.axis_index("table")
+    chips = n // 2
+    core, chip = lax.rem(me, 2), me // 2
+    line = some_rows(core * chips + chip // Y * Y, Y, rows)
+    for o in range(1, chips // Y):
+        remote(dst.at[line], dst.at[line], sems, lax.rem(chip + o * Y, chips) * 2 + core)
+
+
+def core_major(columns):
+    n = columns.shape[1]
+    at = iota((n, n), 1)
+    order = iota((n, n), 0) == lax.rem(at, n // 2) * 2 + at // (n // 2)
+    order = jnp.where(order, 1.0, 0.0).astype(BF16)
+    high, low = columns >> 5, columns & 31
+    return dot(high.astype(BF16), order) * 32.0 + dot(low.astype(BF16), order)
 
 
 def step_kernel(
@@ -157,8 +241,10 @@
     fetched,
     base_own,
     base,
-    state_own,
-    states,
+    demote_base,
+    demote_bases,
+    demote_grad,
+    demote_grads,
     table,
     rows,
     cold_send,
@@ -166,8 +252,8 @@
     cold_back,
     hot_back,
     local,
+    local_send,
     promo_own,
-    demote_own,
     hot_own,
     cold_parts,
     promo_parts,
@@ -176,9 +262,9 @@
     hot_grad,
     promo_grad,
     cold_grad,
-    demoted,
     pick,
     start,
+    total,
     w_sem,
     send_sem,
     recv_sem,
@@ -194,6 +280,9 @@
     blocks = slots // half
     table_got = pl.ds(0, (n - 1) * cap)
     dp_got = groups - 1
+    cells = base_own.shape[0]
+    chips = n // 2
+    sem = [(send_sem.at[i], recv_sem.at[i]) for i in range(send_sem.shape[0])]
 
     load = pltpu.make_async_copy(w_hbm, w_hidden, w_sem)
     load.start()
@@ -206,45 +295,63 @@
     pl.semaphore_wait(barrier, greeted)
     send_blocks("table", served, fetched, cap, True, send_sem.at[0], recv_sem.at[0])
     own_block("table", served, fetched, cap, True)
+    for i in range(pad):
+        demote_base[i : i + 1, :] = replica[pl.ds(demote_slots[0, i], 1), :]
+    demote_base[pad : 2 * pad, :] = column_of(lambda i: hot_state_scalars[0, demote_slots[0, i]], pad, width, F32)
+    send_blocks("dp", demote_base, demote_bases, 2 * pad, False, send_sem.at[2], recv_sem.at[2])
+    own_block("dp", demote_base, demote_bases, 2 * pad, False)
 
     for q in range(blocks):
         table[q * width : (q + 1) * width, :] = replica[q * half : (q + 1) * half, :].T.astype(BF16)
-    for f in range(fields):
-        code = lookups[f : f + 1, :]
+    def field(f):
+        return pl.ds(pl.multiple_of(f * width, width), width)
+
+    def hot_entries(f, carry):
+        code = lookups[pl.ds(f, 1), :]
         found = dot(table[...], one_hot(code & (half - 1), (half, batch), 0))
         block = code >> (half.bit_length() - 1)
         entry = jnp.where(block == 0, found[:width, :], 0.0)
         for q in range(1, blocks):
             entry = jnp.where(block == q, found[q * width : (q + 1) * width, :], entry)
-        rows[f * width : (f + 1) * width, :] = entry.astype(BF16)
+        rows[field(f), :] = entry.astype(BF16)
+        return carry
+
+    lax.fori_loop(0, fields, hot_entries, 0)
     load.wait()
-    for f in range(fields):
-        part = slice(f * width, (f + 1) * width)
-        w_flipped[:, part] = w_hidden[part, :].T
-    head = jnp.broadcast_to(w_head[...].astype(F32), (width, w_head.shape[1])).T
+
+    def flip(f, carry):
+        w_flipped[:, field(f)] = w_hidden[field(f), :].T
+        return carry
+
+    lax.fori_loop(0, fields, flip, 0)
+    head = jnp.broadcast_to(w_head[...].astype(F32).reshape(1, -1), (width, w_head.shape[0])).T
     for i in range(pad):
         base_own[i : i + 1, :] = cold_table[pl.ds(promote_rows[0, i], 1), :]
     place = iota((8, width), 1)
     state = jnp.zeros((8, width), F32)
     for i in range(pad):
         state = jnp.where(place == i, cold_state_scalars[promote_rows[0, i]], state)
-    state_own[...] = state
+    base_own[pad:cells, :] = state
 
     wait_bytes(fetched.at[table_got], recv_sem.at[0])
-    send_blocks("table", base_own, base, pad, False, send_sem.at[1], recv_sem.at[1])
-    send_blocks("table", state_own, states, 8, False, send_sem.at[2], recv_sem.at[2])
-    own_block("table", base_own, base, pad, False)
-    own_block("table", state_own, states, 8, False)
+    gather_along_y(base_own, base, cells, sem[1])
     for q in range(blocks):
         table[q * width : (q + 1) * width, :] = fetched[q * half : (q + 1) * half, :].astype(F32).T.astype(BF16)
-    for f in range(fields):
-        code = lookups[f : f + 1, :]
+
+    def cold_entries(f, carry):
+        code = lookups[pl.ds(f, 1), :]
         found = dot(table[...], one_hot(code & (half - 1), (half, batch), 0))
         block = code >> (half.bit_length() - 1)
-        entry = rows[f * width : (f + 1) * width, :].astype(F32)
+        entry = rows[field(f), :].astype(F32)
         for q in range(blocks):
             entry = jnp.where(block == blocks + q, found[q * width : (q + 1) * width, :], entry)
-        rows[f * width : (f + 1) * width, :] = entry.astype(BF16)
+        rows[field(f), :] = entry.astype(BF16)
+        return carry
+
+    lax.fori_loop(0, fields, cold_entries, 0)
+
+    wait_bytes(base.at[pl.ds(0, (Y - 1) * cells)], recv_sem.at[1])
+    gather_along_x(base, cells, sem[11])
 
     hidden = dot(w_flipped[...], rows[...])
     sig = jax.nn.sigmoid(hidden)
@@ -257,39 +364,41 @@
     rows[...] = dot(w_hidden[...], hidden_grad).astype(BF16)
 
     def summed(first, out):
-        total = jnp.zeros((half, blocks * width), F32)
-        for f in range(fields):
-            code = lookups[f : f + 1, :]
+        total[...] = jnp.zeros_like(total)
+
+        def add(f, carry):
+            code = lookups[pl.ds(f, 1), :]
             block = code >> (half.bit_length() - 1)
-            grad = rows[f * width : (f + 1) * width, :].astype(F32)
+            grad = rows[field(f), :].astype(F32)
             masked = jnp.concatenate(
                 [jnp.where(block == first + q, grad, 0.0).astype(BF16) for q in range(blocks)], axis=0
             )
-            total += dot_lanes(one_hot(code & (half - 1), (half, batch), 0), masked)
+            total[...] += dot_lanes(one_hot(code & (half - 1), (half, batch), 0), masked)
+            return carry
+
+        lax.fori_loop(0, fields, add, 0)
         for q in range(blocks):
             out[q * half : (q + 1) * half, :] = total[:, q * width : (q + 1) * width].astype(BF16)
 
+    wait_bytes(base.at[pl.ds(0, (chips - Y) * cells)], recv_sem.at[11])
+    gather_other_core(base, cells, sem[12])
     summed(blocks, cold_send)
     send_blocks("table", cold_send, cold_back, cap, True, send_sem.at[3], recv_sem.at[3])
     own_block("table", cold_send, cold_back, cap, True)
     summed(0, hot_send)
-    send_blocks("table", hot_send, hot_back, cap, True, send_sem.at[4], recv_sem.at[4])
-    own_block("table", hot_send, hot_back, cap, True)
+    scatter_by_core(hot_send, hot_back, cap, sem[4])
 
     to_rows = one_hot(flat_lanes(wanted.astype(F32).T).astype(I32), (own, n * cap), 0)
     demote_hot = one_hot(column_of(lambda i: demote_slots[0, i], pad, slots, I32), (pad, slots), 1)
-    for i in range(pad):
-        demote_own[i : i + 1, :] = replica[pl.ds(demote_slots[0, i], 1), :]
-    demote_state = column_of(lambda i: hot_state_scalars[0, demote_slots[0, i]], pad, width, F32)
     counts = tile_counts[...]
     live = iota((pad, n), 0) < counts[1:2, :] * TILE
-    targets = flat_lanes(jnp.where(live, promote_slots[...], slots).astype(F32).T).astype(I32)
+    targets = flat_lanes(core_major(jnp.where(live, promote_slots[...], slots)).T).astype(I32)
     pick[...] = one_hot(targets, (slots, n * pad), 0)
-    wait_bytes(base.at[table_got], recv_sem.at[1])
-    wait_bytes(states.at[pl.ds(0, (n - 1) * 8)], recv_sem.at[2])
-    chosen = dot(pick[...], jnp.concatenate(split3(base[...]), axis=1))
+    wait_bytes(base.at[pl.ds(0, chips * cells)], recv_sem.at[12])
+    bases = base[...].reshape(n, cells, width)
+    chosen = dot(pick[...], jnp.concatenate(split3(bases[:, :pad].reshape(n * pad, width)), axis=1))
     picked = (chosen[:, :width] + chosen[:, width : 2 * width]) + chosen[:, 2 * width :]
-    state_lanes = flat_lanes(states[...].reshape(n, 8, width)[:, 0, :pad])
+    state_lanes = flat_lanes(bases[:, pad, :pad])
     pieces = [piece.astype(F32) for piece in split3(state_lanes)]
     side_rows = jnp.concatenate(pieces + [jnp.ones_like(state_lanes)] + [jnp.zeros_like(state_lanes)] * 4, axis=0)
     side = dot_lanes(pick[...], side_rows.astype(BF16))
@@ -300,39 +409,47 @@
 
     wait_bytes(cold_back.at[table_got], recv_sem.at[3])
     local[...] = dot(to_rows, cold_back[...])
-    for i in range(pad):
-        promo_own[i : i + 1, :] = local[pl.ds(promote_rows[0, i], 1), :]
+    promo_own[...] = jnp.concatenate([local[pl.ds(promote_rows[0, i], 1), :] for i in range(pad)], axis=0).astype(BF16)
+    local_send[...] = local[...].astype(BF16)
     send_blocks("dp", promo_own, promo_parts, pad, False, send_sem.at[5], recv_sem.at[5])
-    send_blocks("dp", local, cold_parts, share, True, send_sem.at[6], recv_sem.at[6])
+    send_blocks("dp", local_send, cold_parts, share, True, send_sem.at[6], recv_sem.at[6])
     own_block("dp", promo_own, promo_parts, pad, False)
-    own_block("dp", local, cold_parts, share, True)
+    own_block("dp", local_send, cold_parts, share, True)
     wait_bytes(hot_back.at[table_got], recv_sem.at[4])
     hot_own[...] = jnp.sum(hot_back[...].astype(F32).reshape(n, cap, width), axis=0).astype(BF16)
-    send_blocks("table", hot_own, hot_grad, cap, False, send_sem.at[7], recv_sem.at[7])
-    own_block("table", hot_own, hot_grad, cap, False)
+    gather_same_core(hot_own, hot_grad, cap, sem[7])
     wait_bytes(promo_parts.at[pl.ds(0, dp_got * pad)], recv_sem.at[5])
-    promo_sum[...] = jnp.sum(promo_parts[...].reshape(groups, pad, width), axis=0).astype(BF16)
-    send_blocks("table", promo_sum, promo_grad, pad, False, send_sem.at[8], recv_sem.at[8])
-    own_block("table", promo_sum, promo_grad, pad, False)
+    promo_sum[...] = jnp.sum(promo_parts[...].astype(F32).reshape(groups, pad, width), axis=0).astype(BF16)
+    gather_same_core(promo_sum, promo_grad, pad, sem[8])
     wait_bytes(cold_parts.at[pl.ds(0, dp_got * share)], recv_sem.at[6])
-    cold_own[...] = jnp.sum(cold_parts[...].reshape(groups, share, width), axis=0).astype(BF16)
+    cold_own[...] = jnp.sum(cold_parts[...].astype(F32).reshape(groups, share, width), axis=0).astype(BF16)
     send_blocks("dp", cold_own, cold_grad, share, False, send_sem.at[9], recv_sem.at[9])
     own_block("dp", cold_own, cold_grad, share, False)
-    wait_bytes(hot_grad.at[table_got], recv_sem.at[7])
-    values, renewed = adagrad(demote_own[0:pad, :], demote_state, dot(demote_hot, hot_grad[...]))
-    demote_own[0:pad, :] = values
-    demote_own[pad : 2 * pad, :] = renewed
-    send_blocks("dp", demote_own, demoted, 2 * pad, False, send_sem.at[10], recv_sem.at[10])
-    own_block("dp", demote_own, demoted, 2 * pad, False)
+    core_got = pl.ds(0, (chips - 1) * cap)
+    half_got = pl.ds(0, chips * cap)
+    wait_bytes(hot_grad.at[core_got], recv_sem.at[7])
+    gather_other_core(hot_grad, cap, sem[13])
+    wait_bytes(hot_grad.at[half_got], recv_sem.at[13])
+    demote_grad[...] = dot(demote_hot, hot_grad[...]).astype(BF16)
+    send_blocks("dp", demote_grad, demote_grads, pad, False, send_sem.at[10], recv_sem.at[10])
+    own_block("dp", demote_grad, demote_grads, pad, False)
+    wait_bytes(promo_grad.at[core_got], recv_sem.at[8])
+    gather_other_core(promo_grad, pad, sem[14])
     wait_bytes(cold_grad.at[pl.ds(0, dp_got * share)], recv_sem.at[9])
     values, renewed = adagrad(cold_table[...], cold_column, cold_grad[...].astype(F32))
-    wait_bytes(promo_grad.at[table_got], recv_sem.at[8])
+    wait_bytes(promo_grad.at[half_got], recv_sem.at[14])
     grad = jnp.where(promoted, dot(pick[...], promo_grad[...]), hot_grad[...].astype(F32))
     hot_values, hot_renewed = adagrad(start[...], start_state, grad)
     replica_next[...] = hot_values
     hot_state_next[...] = column_to_lanes(hot_renewed)
-    wait_bytes(demoted.at[pl.ds(0, dp_got * 2 * pad)], recv_sem.at[10])
-    mean = jnp.sum(demoted[...].reshape(groups, 2 * pad, width), axis=0) / groups
+    wait_bytes(demote_bases.at[pl.ds(0, dp_got * 2 * pad)], recv_sem.at[2])
+    wait_bytes(demote_grads.at[pl.ds(0, dp_got * pad)], recv_sem.at[10])
+    mean = jnp.zeros((2 * pad, width), F32)
+    for g in range(groups):
+        old, old_state = demote_bases[2 * pad * g : 2 * pad * g + pad, :], demote_bases[2 * pad * g + pad : 2 * pad * (g + 1), :]
+        new, new_state = adagrad(old, old_state, demote_grads[pad * g : pad * (g + 1), :].astype(F32))
+        mean += jnp.concatenate([new, new_state], axis=0)
+    mean = mean / groups
     renewed = jnp.broadcast_to(renewed, (own, width))
     count = jnp.sum(jnp.where(iota((1, n), 1) == me, counts[0:1, :], 0), axis=1, keepdims=True) * TILE
     row = iota((own, width), 0)
@@ -343,17 +460,32 @@
     cold_next[...] = values
     cold_state_next[...] = renewed.T[:1, :]
 
-    wait_bytes(fetched.at[table_got], send_sem.at[0])
-    wait_bytes(base.at[table_got], send_sem.at[1])
-    wait_bytes(states.at[pl.ds(0, (n - 1) * 8)], send_sem.at[2])
-    wait_bytes(cold_back.at[table_got], send_sem.at[3])
-    wait_bytes(hot_back.at[table_got], send_sem.at[4])
-    wait_bytes(promo_parts.at[pl.ds(0, dp_got * pad)], send_sem.at[5])
-    wait_bytes(cold_parts.at[pl.ds(0, dp_got * share)], send_sem.at[6])
-    wait_bytes(hot_grad.at[table_got], send_sem.at[7])
-    wait_bytes(promo_grad.at[table_got], send_sem.at[8])
-    wait_bytes(cold_grad.at[pl.ds(0, dp_got * share)], send_sem.at[9])
-    wait_bytes(demoted.at[pl.ds(0, dp_got * 2 * pad)], send_sem.at[10])
+    for i, sent in enumerate(
+        (
+            fetched.at[table_got],
+            base.at[pl.ds(0, (Y - 1) * cells)],
+            demote_bases.at[pl.ds(0, dp_got * 2 * pad)],
+            cold_back.at[table_got],
+            hot_back.at[table_got],
+            promo_parts.at[pl.ds(0, dp_got * pad)],
+            cold_parts.at[pl.ds(0, dp_got * share)],
+            hot_grad.at[core_got],
+            promo_grad.at[core_got],
+            cold_grad.at[pl.ds(0, dp_got * share)],
+            demote_grads.at[pl.ds(0, dp_got * pad)],
+            base.at[pl.ds(0, (chips - Y) * cells)],
+            base.at[pl.ds(0, chips * cells)],
+            hot_grad.at[half_got],
+            promo_grad.at[half_got],
+        )
+    ):
+        wait_bytes(sent, send_sem.at[i])
+
+
+def finish_kernel(*refs):
+    count = len(refs) // 2
+    for i in range(count):
+        refs[count + i][...] = refs[i][...]
 
 
 def body(
@@ -381,15 +513,16 @@
     inputs, units = w_hidden.shape
     dma = pltpu.SemaphoreType.DMA
     shape = jax.ShapeDtypeStruct
-    logits, replica_next, hot_state_next, cold_next, cold_state_next = pl.pallas_call(
+    results = (
+        shape((1, batch), F32),
+        shape((slots, width), F32),
+        shape((1, slots), F32),
+        shape((own, width), F32),
+        shape((1, own), F32),
+    )
+    found = pl.pallas_call(
         step_kernel,
-        out_shape=(
-            shape((1, batch), F32),
-            shape((slots, width), F32),
-            shape((1, slots), F32),
-            shape((own, width), F32),
-            shape((1, own), F32),
-        ),
+        out_shape=results,
         in_specs=[smem()] * 5 + [vmem()] * 6 + [pl.BlockSpec(memory_space=pl.ANY)] + [vmem()] * 4,
         out_specs=(vmem(),) * 5,
         scratch_shapes=[
@@ -398,10 +531,12 @@
             pltpu.VMEM((n * cap, own), BF16),
             pltpu.VMEM((n * cap, width), BF16),
             pltpu.VMEM((n * cap, width), BF16),
-            pltpu.VMEM((pad, width), F32),
-            pltpu.VMEM((n * pad, width), F32),
-            pltpu.VMEM((8, width), F32),
-            pltpu.VMEM((n * 8, width), F32),
+            pltpu.VMEM((pad + 8, width), F32),
+            pltpu.VMEM((n * (pad + 8), width), F32),
+            pltpu.VMEM((2 * pad, width), F32),
+            pltpu.VMEM((groups * 2 * pad, width), F32),
+            pltpu.VMEM((pad, width), BF16),
+            pltpu.VMEM((groups * pad, width), BF16),
             pltpu.VMEM((2 * width, 512), BF16),
             pltpu.VMEM((inputs, batch), BF16),
             pltpu.VMEM((n * cap, width), BF16),
@@ -409,22 +544,22 @@
             pltpu.VMEM((n * cap, width), BF16),
             pltpu.VMEM((slots, width), BF16),
             pltpu.VMEM((own, width), F32),
-            pltpu.VMEM((pad, width), F32),
-            pltpu.VMEM((2 * pad, width), F32),
+            pltpu.VMEM((own, width), BF16),
+            pltpu.VMEM((pad, width), BF16),
             pltpu.VMEM((slots // n, width), BF16),
-            pltpu.VMEM((own, width), F32),
-            pltpu.VMEM((groups * pad, width), F32),
+            pltpu.VMEM((own, width), BF16),
+            pltpu.VMEM((groups * pad, width), BF16),
             pltpu.VMEM((own // groups, width), BF16),
             pltpu.VMEM((pad, width), BF16),
             pltpu.VMEM((slots, width), BF16),
             pltpu.VMEM((n * pad, width), BF16),
             pltpu.VMEM((own, width), BF16),
-            pltpu.VMEM((groups * 2 * pad, width), F32),
             pltpu.VMEM((slots, n * pad), BF16),
             pltpu.VMEM((slots, width), F32),
+            pltpu.VMEM((512, 2 * width), F32),
             dma,
-            dma((11,)),
-            dma((11,)),
+            dma((15,)),
+            dma((15,)),
         ],
         compiler_params=pltpu.CompilerParams(collective_id=0, has_side_effects=True, vmem_limit_bytes=LIMIT),
         name="step",
@@ -441,11 +576,19 @@
         cold_table,
         cold_state.reshape(1, own),
         w_hidden,
-        w_head.reshape(1, units),
+        w_head,
         requests.transpose(0, 1, 3, 2),
         tile_counts.T,
         promote_slots.T,
     )
+    logits, replica_next, hot_state_next, cold_next, cold_state_next = pl.pallas_call(
+        finish_kernel,
+        out_shape=results,
+        in_specs=[vmem()] * 5,
+        out_specs=[vmem()] * 5,
+        compiler_params=pltpu.CompilerParams(vmem_limit_bytes=LIMIT),
+        name="finish",
+    )(*found)
     return (logits[0], replica_next[None], hot_state_next, cold_next, cold_state_next[0])
 
 

time: 93.4 us -> 82.7 us (0.89)
  local copies, waits for them, and re-layouts: 8.59 us -> 0 us
  Pallas kernels: 83.8 us -> 81.9 us
    unnamed x5 -> x0, local copies, waits for them, and re-layouts: 7.31 us -> none
    pallas_call x1 -> x2, Pallas kernels: 83.8 us -> 81.9 us  [the longest x1 79.9 us: body(): pl.pallas_call(step_kernel, out_shape=results, in_specs=[smem()] * 5 + [v...]
    reshape x1 -> x0, local copies, waits for them, and re-layouts: 1.28 us -> none  [body(): w_head.reshape(1, units)]
where the time goes in v3:
time: 82.7 us; the launch traced here: 82.6 us
  Pallas kernels  81.9 us (99%)
    pallas_call x1, Pallas kernels, body(): pl.pallas_call(step_kernel, out_shape=results, in_specs=[smem()] * 5 + [v...  79.9 us
    pallas_call x1, Pallas kernels, body(): pl.pallas_call(finish_kernel, out_shape=results, in_specs=[vmem()] * 5, o...  2.02 us

profile of v3, /device:TPU:1, one launch (start us, length us, event | category | flops | bytes accessed | tf_op | source)
XLA Modules:
  0.0 82.6 jit_solution(10103595891956374051)
XLA Ops:
  0.6 79.9 %step.1 = (f32[1,1024]{1,0:T(1,128)}, f32[1024,128]{1,0:T(8,128)}, f32[1,1024]{1,0:T(1,128)}, f32[512,128]{1,0:T(8,128)}, f32[1,512]{1,0:T(1,128)}) custom-call(s32[1,16]{1,0:T(1,128)} %promote_rows.1, s32[1,16]{1,0:T(1,128)} %demote_rows.1, s32[1,16]{1,0:T(1,128)} %demote_slots.1, f32[512]{0:T(512)} %cold_state_scalars.1, f32[1,1024]{1,0:T(1,128)} %hot_state.1, ...), custom_call_target="tpu_custom_call" | custom-call | tf_op jit(solution)/shard_map/step/pallas_call | solution.py:523
  80.5 2.0 %finish.1 = (f32[1,1024]{1,0:T(1,128)}, f32[1024,128]{1,0:T(8,128)}, f32[1,1024]{1,0:T(1,128)}, f32[512,128]{1,0:T(8,128)}, f32[1,512]{1,0:T(1,128)}) custom-call(f32[1,1024]{1,0:T(1,128)} %get-tuple-element.15.refs_0_, f32[1024,128]{1,0:T(8,128)} %get-tuple-element.16.refs_1_, f32[1,1024]{1,0:T(1,128)} %get-tuple-element.17.refs_2_, ...), custom_call_target="tpu_custom_call" | custom-call | tf_op jit(solution)/shard_map/finish/pallas_call | solution.py:584

commit v4 on v3

--- a/solution.py
+++ b/solution.py
@@ -14,6 +14,8 @@
 
 TILE = 8
 RATE = 0.3
+GATHER_FIELDS = 2
+SUM_FIELDS = 6
 LIMIT = 56 * 1024 * 1024
 
 
@@ -306,7 +308,16 @@
     def field(f):
         return pl.ds(pl.multiple_of(f * width, width), width)
 
-    def hot_entries(f, carry):
+    def by_fields(count, step):
+        def some(k, carry):
+            step([k * count + i for i in range(count)])
+            return carry
+
+        lax.fori_loop(0, fields // count, some, 0)
+        if fields % count:
+            step(list(range(fields - fields % count, fields)))
+
+    def hot_entry(f):
         code = lookups[pl.ds(f, 1), :]
         found = dot(table[...], one_hot(code & (half - 1), (half, batch), 0))
         block = code >> (half.bit_length() - 1)
@@ -314,9 +325,8 @@
         for q in range(1, blocks):
             entry = jnp.where(block == q, found[q * width : (q + 1) * width, :], entry)
         rows[field(f), :] = entry.astype(BF16)
-        return carry
-
-    lax.fori_loop(0, fields, hot_entries, 0)
+
+    by_fields(GATHER_FIELDS, lambda some: [hot_entry(f) for f in some])
     load.wait()
 
     def flip(f, carry):
@@ -338,7 +348,7 @@
     for q in range(blocks):
         table[q * width : (q + 1) * width, :] = fetched[q * half : (q + 1) * half, :].astype(F32).T.astype(BF16)
 
-    def cold_entries(f, carry):
+    def cold_entry(f):
         code = lookups[pl.ds(f, 1), :]
         found = dot(table[...], one_hot(code & (half - 1), (half, batch), 0))
         block = code >> (half.bit_length() - 1)
@@ -346,9 +356,8 @@
         for q in range(blocks):
             entry = jnp.where(block == blocks + q, found[q * width : (q + 1) * width, :], entry)
         rows[field(f), :] = entry.astype(BF16)
-        return carry
-
-    lax.fori_loop(0, fields, cold_entries, 0)
+
+    by_fields(GATHER_FIELDS, lambda some: [cold_entry(f) for f in some])
 
     wait_bytes(base.at[pl.ds(0, (Y - 1) * cells)], recv_sem.at[1])
     gather_along_x(base, cells, sem[11])
@@ -366,17 +375,18 @@
     def summed(first, out):
         total[...] = jnp.zeros_like(total)
 
-        def add(f, carry):
-            code = lookups[pl.ds(f, 1), :]
-            block = code >> (half.bit_length() - 1)
-            grad = rows[field(f), :].astype(F32)
-            masked = jnp.concatenate(
-                [jnp.where(block == first + q, grad, 0.0).astype(BF16) for q in range(blocks)], axis=0
-            )
-            total[...] += dot_lanes(one_hot(code & (half - 1), (half, batch), 0), masked)
-            return carry
-
-        lax.fori_loop(0, fields, add, 0)
+        def add(some):
+            picks, grads = [], []
+            for f in some:
+                code = lookups[pl.ds(f, 1), :]
+                block = code >> (half.bit_length() - 1)
+                grad = rows[field(f), :]
+                keep = [jnp.where(block == first + q, 1.0, 0.0).astype(BF16) for q in range(blocks)]
+                grads.append(jnp.concatenate([grad * mask for mask in keep], axis=0))
+                picks.append(one_hot(code & (half - 1), (half, batch), 0))
+            total[...] += dot_lanes(jnp.concatenate(picks, axis=1), jnp.concatenate(grads, axis=1))
+
+        by_fields(SUM_FIELDS, add)
         for q in range(blocks):
             out[q * half : (q + 1) * half, :] = total[:, q * width : (q + 1) * width].astype(BF16)
 
@@ -394,18 +404,6 @@
     live = iota((pad, n), 0) < counts[1:2, :] * TILE
     targets = flat_lanes(core_major(jnp.where(live, promote_slots[...], slots)).T).astype(I32)
     pick[...] = one_hot(targets, (slots, n * pad), 0)
-    wait_bytes(base.at[pl.ds(0, chips * cells)], recv_sem.at[12])
-    bases = base[...].reshape(n, cells, width)
-    chosen = dot(pick[...], jnp.concatenate(split3(bases[:, :pad].reshape(n * pad, width)), axis=1))
-    picked = (chosen[:, :width] + chosen[:, width : 2 * width]) + chosen[:, 2 * width :]
-    state_lanes = flat_lanes(bases[:, pad, :pad])
-    pieces = [piece.astype(F32) for piece in split3(state_lanes)]
-    side_rows = jnp.concatenate(pieces + [jnp.ones_like(state_lanes)] + [jnp.zeros_like(state_lanes)] * 4, axis=0)
-    side = dot_lanes(pick[...], side_rows.astype(BF16))
-    promoted = side[:, 3:4] > 0.0
-    start[...] = jnp.where(promoted, picked, replica[...])
-    start_state = jnp.where(promoted, (side[:, 0:1] + side[:, 1:2]) + side[:, 2:3], lanes_to_column(hot_state[...]))
-    cold_column = lanes_to_column(cold_state[...])
 
     wait_bytes(cold_back.at[table_got], recv_sem.at[3])
     local[...] = dot(to_rows, cold_back[...])
@@ -425,6 +423,18 @@
     cold_own[...] = jnp.sum(cold_parts[...].astype(F32).reshape(groups, share, width), axis=0).astype(BF16)
     send_blocks("dp", cold_own, cold_grad, share, False, send_sem.at[9], recv_sem.at[9])
     own_block("dp", cold_own, cold_grad, share, False)
+    wait_bytes(base.at[pl.ds(0, chips * cells)], recv_sem.at[12])
+    bases = base[...].reshape(n, cells, width)
+    chosen = dot(pick[...], jnp.concatenate(split3(bases[:, :pad].reshape(n * pad, width)), axis=1))
+    picked = (chosen[:, :width] + chosen[:, width : 2 * width]) + chosen[:, 2 * width :]
+    state_lanes = flat_lanes(bases[:, pad, :pad])
+    pieces = [piece.astype(F32) for piece in split3(state_lanes)]
+    side_rows = jnp.concatenate(pieces + [jnp.ones_like(state_lanes)] + [jnp.zeros_like(state_lanes)] * 4, axis=0)
+    side = dot_lanes(pick[...], side_rows.astype(BF16))
+    promoted = side[:, 3:4] > 0.0
+    start[...] = jnp.where(promoted, picked, replica[...])
+    start_state = jnp.where(promoted, (side[:, 0:1] + side[:, 1:2]) + side[:, 2:3], lanes_to_column(hot_state[...]))
+    cold_column = lanes_to_column(cold_state[...])
     core_got = pl.ds(0, (chips - 1) * cap)
     half_got = pl.ds(0, chips * cap)
     wait_bytes(hot_grad.at[core_got], recv_sem.at[7])

time: 82.7 us -> 78.5 us (0.949)
  Pallas kernels: 81.9 us -> 77.7 us
    pallas_call x1, Pallas kernels: 79.9 us -> 75.7 us  [body(): pl.pallas_call(step_kernel, out_shape=results, in_specs=[smem()] * 5 + [v...]
where the time goes in v4:
time: 78.5 us; the launch traced here: 78.4 us
  Pallas kernels  77.7 us (99%)
    pallas_call x1, Pallas kernels, body(): pl.pallas_call(step_kernel, out_shape=results, in_specs=[smem()] * 5 + [v...  75.7 us
    pallas_call x1, Pallas kernels, body(): pl.pallas_call(finish_kernel, out_shape=results, in_specs=[vmem()] * 5, o...  2.02 us

profile of v4, /device:TPU:1, one launch (start us, length us, event | category | flops | bytes accessed | tf_op | source)
XLA Modules:
  0.0 78.4 jit_solution(13916562845296220836)
XLA Ops:
  0.6 75.7 %step.1 = (f32[1,1024]{1,0:T(1,128)}, f32[1024,128]{1,0:T(8,128)}, f32[1,1024]{1,0:T(1,128)}, f32[512,128]{1,0:T(8,128)}, f32[1,512]{1,0:T(1,128)}) custom-call(s32[1,16]{1,0:T(1,128)} %promote_rows.1, s32[1,16]{1,0:T(1,128)} %demote_rows.1, s32[1,16]{1,0:T(1,128)} %demote_slots.1, f32[512]{0:T(512)} %cold_state_scalars.1, f32[1,1024]{1,0:T(1,128)} %hot_state.1, ...), custom_call_target="tpu_custom_call" | custom-call | tf_op jit(solution)/shard_map/step/pallas_call | solution.py:533
  76.3 2.0 %finish.1 = (f32[1,1024]{1,0:T(1,128)}, f32[1024,128]{1,0:T(8,128)}, f32[1,1024]{1,0:T(1,128)}, f32[512,128]{1,0:T(8,128)}, f32[1,512]{1,0:T(1,128)}) custom-call(f32[1,1024]{1,0:T(1,128)} %get-tuple-element.15.refs_0_, f32[1024,128]{1,0:T(8,128)} %get-tuple-element.16.refs_1_, f32[1,1024]{1,0:T(1,128)} %get-tuple-element.17.refs_2_, ...), custom_call_target="tpu_custom_call" | custom-call | tf_op jit(solution)/shard_map/finish/pallas_call | solution.py:594

commit v5 on v4

--- a/solution.py
+++ b/solution.py
@@ -400,10 +400,6 @@
 
     to_rows = one_hot(flat_lanes(wanted.astype(F32).T).astype(I32), (own, n * cap), 0)
     demote_hot = one_hot(column_of(lambda i: demote_slots[0, i], pad, slots, I32), (pad, slots), 1)
-    counts = tile_counts[...]
-    live = iota((pad, n), 0) < counts[1:2, :] * TILE
-    targets = flat_lanes(core_major(jnp.where(live, promote_slots[...], slots)).T).astype(I32)
-    pick[...] = one_hot(targets, (slots, n * pad), 0)
 
     wait_bytes(cold_back.at[table_got], recv_sem.at[3])
     local[...] = dot(to_rows, cold_back[...])
@@ -423,6 +419,10 @@
     cold_own[...] = jnp.sum(cold_parts[...].astype(F32).reshape(groups, share, width), axis=0).astype(BF16)
     send_blocks("dp", cold_own, cold_grad, share, False, send_sem.at[9], recv_sem.at[9])
     own_block("dp", cold_own, cold_grad, share, False)
+    counts = tile_counts[...]
+    live = iota((pad, n), 0) < counts[1:2, :] * TILE
+    targets = flat_lanes(core_major(jnp.where(live, promote_slots[...], slots)).T).astype(I32)
+    pick[...] = one_hot(targets, (slots, n * pad), 0)
     wait_bytes(base.at[pl.ds(0, chips * cells)], recv_sem.at[12])
     bases = base[...].reshape(n, cells, width)
     chosen = dot(pick[...], jnp.concatenate(split3(bases[:, :pad].reshape(n * pad, width)), axis=1))

time: 78.5 us -> 78.6 us (level)
  no operation moved by 1% of the time
where the time goes in v5:
time: 78.6 us; the launch traced here: 78.4 us
  Pallas kernels  77.8 us (99%)
    pallas_call x1, Pallas kernels, body(): pl.pallas_call(step_kernel, out_shape=results, in_specs=[smem()] * 5 + [v...  75.8 us
    pallas_call x1, Pallas kernels, body(): pl.pallas_call(finish_kernel, out_shape=results, in_specs=[vmem()] * 5, o...  2.02 us

profile of v5, /device:TPU:1, one launch (start us, length us, event | category | flops | bytes accessed | tf_op | source)
XLA Modules:
  0.0 78.4 jit_solution(15505519792783822936)
XLA Ops:
  0.6 75.8 %step.1 = (f32[1,1024]{1,0:T(1,128)}, f32[1024,128]{1,0:T(8,128)}, f32[1,1024]{1,0:T(1,128)}, f32[512,128]{1,0:T(8,128)}, f32[1,512]{1,0:T(1,128)}) custom-call(s32[1,16]{1,0:T(1,128)} %promote_rows.1, s32[1,16]{1,0:T(1,128)} %demote_rows.1, s32[1,16]{1,0:T(1,128)} %demote_slots.1, f32[512]{0:T(512)} %cold_state_scalars.1, f32[1,1024]{1,0:T(1,128)} %hot_state.1, ...), custom_call_target="tpu_custom_call" | custom-call | tf_op jit(solution)/shard_map/step/pallas_call | solution.py:533
  76.4 2.0 %finish.1 = (f32[1,1024]{1,0:T(1,128)}, f32[1024,128]{1,0:T(8,128)}, f32[1,1024]{1,0:T(1,128)}, f32[512,128]{1,0:T(8,128)}, f32[1,512]{1,0:T(1,128)}) custom-call(f32[1,1024]{1,0:T(1,128)} %get-tuple-element.15.refs_0_, f32[1024,128]{1,0:T(8,128)} %get-tuple-element.16.refs_1_, f32[1,1024]{1,0:T(1,128)} %get-tuple-element.17.refs_2_, ...), custom_call_target="tpu_custom_call" | custom-call | tf_op jit(solution)/shard_map/finish/pallas_call | solution.py:594
